TPU v7x, 512 devices: a whole 4x4x16 slice. The times are simulated.
512 devices in a mesh: dp: 64 (over y, z), seq: 8 (over x, core).
Axes of the slice: x: 4, y: 4, z: 16, core: 2. Of those that a mesh axis runs over, the one named last changes fastest.
Arguments:
- queries: bfloat16 [131072, 768], P(('dp', 'seq')), may hold values from -160 to 160
- keys: bfloat16 [131072, 768], P(('dp', 'seq')), may hold values from -4 to 4
- values: bfloat16 [131072, 768], P(('dp', 'seq')), may hold values from -6 to 6
- out_grad: bfloat16 [131072, 768], P(('dp', 'seq')), may hold values from -24 to 24
- out_weight: bfloat16 [768, 768], replicated, may hold values from -0.21875 to 0.21875
- slide_lengths: int32 [64, 4], P('dp'), may hold values from 1 to 1024, 2048 in all within a row
Outputs:
- query_grad: bfloat16 [131072, 768], P(('dp', 'seq'))
- key_grad: bfloat16 [131072, 768], P(('dp', 'seq'))
- value_grad: bfloat16 [131072, 768], P(('dp', 'seq'))
- weight_grad: float32 [768, 768], P('dp', 'seq')
Inputs may be any that keep to these rules, and one draw needn't show every extreme that they name: `slide_lengths`: the 4 lengths of a group sum to 2048; the longest of each group is exactly 1024.
All inputs are finite; a program needn't handle non-finite values.
Results may differ from a plain program's by a relative error of at most 0.023.
Values may be sent and summed in bfloat16 or wider, within the bound.
A program may use at most 64 MiB of HBM per device.

v0:
```python
import jax
import jax.numpy as jnp
from jax import lax
from jax.sharding import PartitionSpec as P

NHEAD = 16
SEG = 256


def masked_scores(query, key_rows, ids_q, ids_k):
    scores = jnp.einsum("cqhd,ckhd->cqhk", query, key_rows, preferred_element_type=jnp.float32)
    scores = scores * query.shape[-1] ** (-0.5)
    same = ids_q[:, :, None, None] == ids_k[:, None, None, :]
    return jnp.where(same, scores, -jnp.inf)


def attend_forward(query, key_rows, value_rows, ids_q, ids_k):
    scores = masked_scores(query, key_rows, ids_q, ids_k)
    top = jnp.max(scores, -1, keepdims=True)
    expo = jnp.exp(scores - top)
    total = jnp.sum(expo, -1, keepdims=True)
    weights = (expo / total).astype(jnp.bfloat16)
    out = jnp.einsum("cqhk,ckhd->cqhd", weights, value_rows, preferred_element_type=jnp.float32)
    return (out, top[..., 0] + jnp.log(total[..., 0]))


def attend_backward(query, key_rows, value_rows, ids_q, ids_k, dout, lse, delta):
    scale = query.shape[-1] ** (-0.5)
    scores = masked_scores(query, key_rows, ids_q, ids_k)
    prob = jnp.exp(scores - lse[..., None])
    dvalue = jnp.einsum(
        "cqhk,cqhd->ckhd", prob.astype(jnp.bfloat16), dout, preferred_element_type=jnp.float32
    )
    dprob = jnp.einsum("cqhd,ckhd->cqhk", dout, value_rows, preferred_element_type=jnp.float32)
    dscore = (prob * (dprob - delta[..., None]) * scale).astype(jnp.bfloat16)
    dquery = jnp.einsum("cqhk,ckhd->cqhd", dscore, key_rows, preferred_element_type=jnp.float32)
    dkey = jnp.einsum("cqhk,cqhd->ckhd", dscore, query, preferred_element_type=jnp.float32)
    return (dquery, dkey, dvalue)


def pick(array, spread):
    count, heads, inner = array.shape
    split = array.reshape(count // spread, spread, heads // spread, spread, inner)
    return jnp.stack([split[:, j, :, j, :] for j in range(spread)], 0)


def place(array, spread):
    moved = jnp.transpose(array, (1, 2, 0, 3))
    eye = jnp.eye(spread, dtype=array.dtype)
    full = eye[None, :, None, :, None] * moved[:, None, :, :, :]
    count = moved.shape[0]
    return full.reshape(count * spread, moved.shape[1] * spread, moved.shape[3])


def combine(out_a, lse_a, out_b, lse_b):
    lse = jnp.logaddexp(lse_a, lse_b)
    return (jnp.exp(lse_a - lse)[..., None] * out_a + jnp.exp(lse_b - lse)[..., None] * out_b, lse)


def row_delta(dout, out_rows):
    rounded = lax.optimization_barrier(out_rows.astype(jnp.bfloat16))
    return jnp.sum(dout.astype(jnp.float32) * rounded.astype(jnp.float32), -1)


def on_device(queries, keys, values, out_grad, out_weight, slide_lengths):
    rows_here, width = queries.shape
    spread = lax.axis_size("seq")
    seq_pos = lax.axis_index("seq")
    head_dim = width // NHEAD
    per_class = rows_here // spread
    ends = jnp.cumsum(slide_lengths[0])

    def slide_of(positions):
        return jnp.sum((positions[..., None] >= ends).astype(jnp.int32), -1)

    local_ids = slide_of(seq_pos * rows_here + jnp.arange(rows_here, dtype=jnp.int32))
    dout = lax.dot_general(
        out_grad, out_weight, (((1,), (1,)), ((), ())), preferred_element_type=jnp.float32
    ).astype(jnp.bfloat16)
    q3 = queries.reshape(rows_here, NHEAD, head_dim)
    k3 = keys.reshape(rows_here, NHEAD, head_dim)
    v3 = values.reshape(rows_here, NHEAD, head_dim)
    d3 = dout.reshape(rows_here, NHEAD, head_dim)
    blocks = rows_here // SEG

    def blocked(array):
        return array.reshape(blocks, SEG, NHEAD, array.shape[-1])

    ids_block = local_ids.reshape(blocks, SEG)
    out_a, lse_a = attend_forward(blocked(q3), blocked(k3), blocked(v3), ids_block, ids_block)
    out_a = out_a.reshape(rows_here, NHEAD, head_dim)
    lse_a = lse_a.reshape(rows_here, NHEAD)
    q_sel, k_sel, v_sel, d_sel = (
        pick(q3, spread),
        pick(k3, spread),
        pick(v3, spread),
        pick(d3, spread),
    )
    out_a_sel = pick(out_a, spread)
    lse_a_sel = pick(lse_a[..., None], spread)[..., 0]
    ids_sel = local_ids.reshape(per_class, spread).T
    member = jnp.arange(rows_here, dtype=jnp.int32)
    member_pos = member // per_class * rows_here + member % per_class * spread
    gathered_k, gathered_v = (
        lax.all_gather(k_sel, "seq", axis=1, tiled=True),
        lax.all_gather(v_sel, "seq", axis=1, tiled=True),
    )
    ids_k = slide_of(member_pos[None, :] + jnp.arange(spread, dtype=jnp.int32)[:, None])
    out_b, lse_b = attend_forward(q_sel, gathered_k, gathered_v, ids_sel, ids_k)
    out_c, lse_c = combine(out_a_sel, lse_a_sel, out_b, lse_b)
    delta_c = row_delta(d_sel, out_c)
    dq_b, dk_all, dv_all = attend_backward(
        q_sel, gathered_k, gathered_v, ids_sel, ids_k, d_sel, lse_c, delta_c
    )
    dk_b, dv_b = (
        lax.psum_scatter(dk_all, "seq", scatter_dimension=1, tiled=True),
        lax.psum_scatter(dv_all, "seq", scatter_dimension=1, tiled=True),
    )
    chosen = place(jnp.ones(lse_c.shape + (1,), jnp.float32), spread) > 0.5
    out_full = jnp.where(chosen, place(out_c, spread), out_a)
    lse_full = jnp.where(chosen[..., 0], place(lse_c[..., None], spread)[..., 0], lse_a)
    attended = out_full.astype(jnp.bfloat16)
    delta = jnp.sum(
        d3.astype(jnp.float32) * lax.optimization_barrier(attended).astype(jnp.float32), -1
    )
    dq_a, dk_a, dv_a = attend_backward(
        blocked(q3),
        blocked(k3),
        blocked(v3),
        ids_block,
        ids_block,
        blocked(d3),
        lse_full.reshape(blocks, SEG, NHEAD),
        delta.reshape(blocks, SEG, NHEAD),
    )
    query_grad = (
        (dq_a.reshape(rows_here, NHEAD, head_dim) + place(dq_b, spread))
        .astype(jnp.bfloat16)
        .reshape(rows_here, width)
    )
    key_grad = (
        (dk_a.reshape(rows_here, NHEAD, head_dim) + place(dk_b, spread))
        .astype(jnp.bfloat16)
        .reshape(rows_here, width)
    )
    value_grad = (
        (dv_a.reshape(rows_here, NHEAD, head_dim) + place(dv_b, spread))
        .astype(jnp.bfloat16)
        .reshape(rows_here, width)
    )
    attended_flat = attended.reshape(rows_here, width)
    rows_mine = lax.psum_scatter(
        lax.dot_general(
            attended_flat, out_grad, (((0,), (0,)), ((), ())), preferred_element_type=jnp.float32
        ),
        "dp",
        scatter_dimension=0,
        tiled=True,
    )
    weight_grad = lax.psum_scatter(rows_mine, "seq", scatter_dimension=1, tiled=True)
    return (query_grad, key_grad, value_grad, weight_grad)


def solution(mesh):
    placed = (
        P(("dp", "seq"), None),
        P(("dp", "seq"), None),
        P(("dp", "seq"), None),
        P(("dp", "seq"), None),
        P(),
        P("dp", None),
    )
    return jax.shard_map(
        on_device,
        mesh=mesh,
        in_specs=placed,
        out_specs=(
            P(("dp", "seq"), None),
            P(("dp", "seq"), None),
            P(("dp", "seq"), None),
            P("dp", "seq"),
        ),
        check_vma=False,
    )
```

profile of v0, /device:TPU:1, one launch (start us, length us, event | category | flops | bytes accessed | tf_op | source)
XLA Modules:
  0.0 494.5 jit_solution(7184403988519099359)
XLA Ops:
  8.5 1.2 copy.250
  9.7 3.1 reshape_reshape.11
  14.0 3.1 reshape_reshape.10
  18.0 2.2 reshape_reshape.25
  23.9 2.2 fusion.48
  26.1 1.6 fusion.49
  27.8 20.6 %all_gather.6 = bf16[8,256,2,48]{3,1,2,0:T(8,128)(2,1)S(1)} all-gather(bf16[8,32,2,48]{3,1,2,0:T(8,128)(2,1)S(1)} %constant_dynamic-update-slice_fusion.8), channel_id=1, replica_groups=mesh['dp'=64,'seq'=8] {'seq'}, dimensions={1}, use_global_device_ids=true | all-gather | bytes 442368 | tf_op jit(solution)/shard_map/all_gather | solution.py:105
  48.4 1.9 fusion.50
  50.5 15.0 %all_gather.7 = bf16[8,256,2,48]{3,1,2,0:T(8,128)(2,1)} all-gather(bf16[8,32,2,48]{3,1,2,0:T(8,128)(2,1)S(1)} %constant_dynamic-update-slice_fusion.40), channel_id=1, replica_groups=mesh['dp'=64,'seq'=8] {'seq'}, dimensions={1}, use_global_device_ids=true | all-gather | bytes 442368 | tf_op jit(solution)/shard_map/all_gather | solution.py:106
  66.4 1.9 copy-done.1
  70.7 3.4 fusion.12
  75.2 2.5 copy.273
  77.7 1.7 fusion.46
  83.5 1.2 constant_dynamic-update-slice_fusion.30
  84.8 1.3 constant_dynamic-update-slice_fusion.29
  89.5 1.2 constant_dynamic-update-slice_fusion.25
  90.8 1.2 constant_dynamic-update-slice_fusion.24
  92.9 2.2 fusion.52
  95.5 1.8 mul.257
  97.3 3.6 fusion.29
  100.9 135.7 %fusion = f32[16,768]{1,0:T(8,128)S(1)} fusion(f32[768,768]{1,0:T(8,128)} %fusion.29), kind=kCustom, calls=%all-reduce-scatter | all-reduce-scatter fusion | flops 786433 | bytes 2410496
  236.6 1.9 collective-permute-start.14
  238.5 1.9 collective-permute-start.13
  240.4 1.9 collective-permute-start.12
  242.3 1.9 collective-permute-start.11
  244.8 1.9 collective-permute-start.15
  246.7 2.2 convolution_convert_fusion
  249.0 2.9 reshape_reshape.26
  251.9 1.6 fusion.47
  253.5 1.3 collective-permute-start.10
  254.9 13.4 %collective-permute-start.9 = (f32[16,768]{1,0:T(8,128)S(1)}, f32[16,768]{1,0:T(8,128)S(1)}, u32[]{:S(2)}, u32[]{:S(2)}) collective-permute-start(f32[16,768]{1,0:T(8,128)S(1)} %fusion), channel_id=1, source_target_pairs={{0,80},{8,88},{16,96},{24,104},{32,112},{40,120},{48,128},{56,136}... | collective-permute-start | bytes 147464
  268.3 1.9 collective-permute-start.8
  270.2 10.5 %collective-permute-start.7 = (f32[16,768]{1,0:T(8,128)S(1)}, f32[16,768]{1,0:T(8,128)S(1)}, u32[]{:S(2)}, u32[]{:S(2)}) collective-permute-start(f32[16,768]{1,0:T(8,128)S(1)} %fusion), channel_id=1, source_target_pairs={{0,64},{8,72},{16,80},{24,88},{32,96},{40,104},{48,112},{56,120},{... | collective-permute-start | bytes 147464
  280.8 1.3 collective-permute-start.6
  282.1 7.3 %collective-permute-start.5 = (f32[16,768]{1,0:T(8,128)S(1)}, f32[16,768]{1,0:T(8,128)S(1)}, u32[]{:S(2)}, u32[]{:S(2)}) collective-permute-start(f32[16,768]{1,0:T(8,128)S(1)} %fusion), channel_id=1, source_target_pairs={{0,48},{8,56},{16,64},{24,72},{32,80},{40,88},{48,96},{56,104},{64... | collective-permute-start | bytes 147464
  289.4 1.3 collective-permute-start.4
  290.7 5.6 %collective-permute-start.3 = (f32[16,768]{1,0:T(8,128)S(1)}, f32[16,768]{1,0:T(8,128)}, u32[]{:S(2)}, u32[]{:S(2)}) collective-permute-start(f32[16,768]{1,0:T(8,128)S(1)} %fusion), channel_id=1, source_target_pairs={{0,32},{8,40},{16,48},{24,56},{32,64},{40,72},{48,80},{56,88},{64,... | collective-permute-start | bytes 147464
  296.4 4.8 collective-permute-start.2
  301.2 1.9 collective-permute-start.1
  303.1 2.9 collective-permute-start
  306.0 1.4 dynamic-slice.4
  308.1 25.0 %concatenate.36 = f32[268,768]{1,0:T(8,128)} concatenate(f32[12,768]{1,0:T(8,128)} %collective-permute-done.15, f32[16,768]{1,0:T(8,128)} %collective-permute-done.14, f32[16,768]{1,0:T(8,128)} %collective-permute-done.13, f32[16,768]{1,0:T(8,128)} %collective-permute-done.12, f32[16,768]{1,0:T(8,128)} %collective-permute-done.11, f32[16,768]{1,0:T(8,128)} %copy-done.24, ...), dimensions={0} | concatenate | bytes 1646592
  335.0 2.4 convolution_bitcast_fusion
  337.4 3.6 copy.309
  342.1 1.9 fusion.23
  346.0 3.6 copy.305
  349.6 1.9 copy.269
  353.5 4.1 fusion.14
  358.6 2.4 copy.311
  362.1 1.9 copy.291
  364.0 1.5 fusion.26
  366.7 4.0 fusion.3
  370.7 1.4 fusion.10
  372.1 2.3 copy.303
  374.4 2.6 fusion.8
  377.0 2.3 copy.307
  379.5 1.8 mul.249
  381.3 13.4 %reduce-scatter.12.cloned.1.call-done = f32[96,12]{1,0:T(8,128)} async-done(((f32[768,12]{1,0:T(8,128)}), f32[96,12]{1,0:T(8,128)}) %reduce-scatter.12.cloned.1.call-update) | async-done | bytes 4624
  394.7 1.5 copy.321
  396.2 41.7 %reduce-scatter.10.cloned.1.call-done = f32[8,32,2,48]{3,0,2,1:T(8,128)} async-done(((f32[8,256,2,48]{3,0,2,1:T(8,128)}), f32[8,32,2,48]{3,0,2,1:T(8,128)}) %reduce-scatter.10.cloned.1.call-update) | async-done | bytes 98320 | tf_op jit(solution)/shard_map/reduce_scatter | solution.py:117
  439.1 1.8 mul.255
  440.9 40.3 %reduce-scatter.8.cloned.1.call-done = f32[8,32,2,48]{3,0,2,1:T(8,128)} async-done(((f32[8,256,2,48]{3,0,2,1:T(8,128)}), f32[8,32,2,48]{3,0,2,1:T(8,128)}) %reduce-scatter.8.cloned.1.call-update) | async-done | bytes 98320 | tf_op jit(solution)/shard_map/reduce_scatter | solution.py:116
  482.3 1.8 mul.252
  484.1 3.8 add_convert_fusion
  (203 shorter events, 33.3 us)
Async XLA Ops:
  7.2 239.5 %copy-start = (bf16[768,768]{1,0:T(8,128)(2,1)S(1)}, bf16[768,768]{1,0:T(8,128)(2,1)}, u32[]{:S(2)}) copy-start(bf16[768,768]{1,0:T(8,128)(2,1)} %param.10) | copy-start | bytes 3538948
  7.2 9.9 %copy-start.9 = (bf16[256,768]{1,0:T(8,128)(2,1)S(1)}, bf16[256,768]{1,0:T(8,128)(2,1)}, u32[]{:S(2)}) copy-start(bf16[256,768]{1,0:T(8,128)(2,1)} %param.8) | copy-start | bytes 1179652
  7.2 387.6 %reduce-scatter.12.cloned.1.call-start = ((), (), s32[]{:S(2)}) async-start(), calls=%async_computation.5 | async-start | bytes 442368
  8.5 62.2 %copy-start.14 = (pred[256,256]{0,1:T(8,128)(4,1)}, pred[256,256]{0,1:T(8,128)(4,1)S(1)}, u32[]{:S(2)}) copy-start(pred[256,256]{0,1:T(8,128)(4,1)S(1)} %broadcast_compare_fusion.1) | copy-start | bytes 196612
  9.7 55.8 %copy-start.6 = (bf16[256,768]{0,1:T(8,128)(2,1)}, bf16[256,768]{0,1:T(8,128)(2,1)S(1)}, u32[]{:S(2)}) copy-start(bf16[256,768]{0,1:T(8,128)(2,1)S(1)} %copy.250) | copy-start | bytes 1179652
  14.0 51.5 %copy-start.7 = (bf16[256,768]{0,1:T(8,128)(2,1)}, bf16[256,768]{0,1:T(8,128)(2,1)S(1)}, u32[]{:S(2)}) copy-start(bf16[256,768]{0,1:T(8,128)(2,1)S(1)} %copy.249) | copy-start | bytes 1179652
  21.8 0.6 copy-start.30
  48.4 34.2 %copy-start.2 = (bf16[8,256,2,48]{3,1,2,0:T(8,128)(2,1)}, bf16[8,256,2,48]{3,1,2,0:T(8,128)(2,1)S(1)}, u32[]{:S(2)}) copy-start(bf16[8,256,2,48]{3,1,2,0:T(8,128)(2,1)S(1)} %all_gather.6) | copy-start | bytes 1179652
  66.3 1.9 copy-start.1
  69.2 5.0 %copy-start.17 = (f32[256,16]{0,1:T(8,128)}, f32[256,16]{0,1:T(8,128)S(1)}, u32[]{:S(2)}) copy-start(f32[256,16]{0,1:T(8,128)S(1)} %log_add_fusion) | copy-start | bytes 49156
  70.2 4.0 copy-start.39
  74.2 20.9 %copy-start.4 = (f32[16,256,48]{1,2,0:T(8,128)}, f32[16,256,48]{1,2,0:T(8,128)S(1)}, u32[]{:S(2)}) copy-start(f32[16,256,48]{1,2,0:T(8,128)S(1)} %fusion.12) | copy-start | bytes 2359300
  74.2 8.4 %copy-start.21 = (bf16[32,1,2,1,48]{4,3,2,1,0:T(2,128)(2,1)S(1)}, bf16[32,1,2,1,48]{4,3,2,1,0:T(2,128)(2,1)}, u32[]{:S(2)}) copy-start(bf16[32,1,2,1,48]{4,3,2,1,0:T(2,128)(2,1)} %get-tuple-element.32) | copy-start | bytes 18436
  74.2 8.4 %copy-start.20 = (bf16[32,1,2,1,48]{4,3,2,1,0:T(2,128)(2,1)S(1)}, bf16[32,1,2,1,48]{4,3,2,1,0:T(2,128)(2,1)}, u32[]{:S(2)}) copy-start(bf16[32,1,2,1,48]{4,3,2,1,0:T(2,128)(2,1)} %get-tuple-element.31) | copy-start | bytes 18436
  74.2 8.3 %copy-start.22 = (bf16[32,1,2,1,48]{4,3,2,1,0:T(2,128)(2,1)S(1)}, bf16[32,1,2,1,48]{4,3,2,1,0:T(2,128)(2,1)}, u32[]{:S(2)}) copy-start(bf16[32,1,2,1,48]{4,3,2,1,0:T(2,128)(2,1)} %get-tuple-element.33) | copy-start | bytes 18436
  82.7 12.5 %copy-start.12 = (bf16[8,32,2,48]{3,1,2,0:T(8,128)(2,1)}, bf16[8,32,2,48]{3,1,2,0:T(8,128)(2,1)S(1)}, u32[]{:S(2)}) copy-start(bf16[8,32,2,48]{3,1,2,0:T(8,128)(2,1)S(1)} %constant_dynamic-update-slice_fusion.16) | copy-start | bytes 147460
  83.2 11.9 %copy-start.5 = (f32[8,32,2,256]{3,1,2,0:T(8,128)}, f32[8,32,2,256]{3,1,2,0:T(8,128)S(1)}, u32[]{:S(2)}) copy-start(f32[8,32,2,256]{3,1,2,0:T(8,128)S(1)} %get-tuple-element.60) | copy-start | bytes 1572868
  83.2 11.9 %copy-start.15 = (f32[8,32,2]{1,2,0:T(2,128)}, f32[8,32,2]{1,2,0:T(2,128)S(1)}, u32[]{:S(2)}) copy-start(f32[8,32,2]{1,2,0:T(2,128)S(1)} %get-tuple-element.59) | copy-start | bytes 6148
  83.5 13.8 %copy-start.18 = (f32[8,32,2]{1,2,0:T(2,128)}, f32[8,32,2]{1,2,0:T(2,128)S(1)}, u32[]{:S(2)}) copy-start(f32[8,32,2]{1,2,0:T(2,128)S(1)} %fusion.27) | copy-start | bytes 6148
  92.8 4.6 copy-start.23
  236.6 18.3 %collective-permute-start.14 = (f32[16,768]{1,0:T(8,128)S(1)}, f32[16,768]{1,0:T(8,128)}, u32[]{:S(2)}, u32[]{:S(2)}) collective-permute-start(f32[16,768]{1,0:T(8,128)S(1)} %fusion), channel_id=1, source_target_pairs={{0,120},{8,128},{16,136},{24,144},{32,152},{40,160},{48,168},{56,1... | collective-permute-start | bytes 147464
  238.5 29.8 %collective-permute-start.13 = (f32[16,768]{1,0:T(8,128)S(1)}, f32[16,768]{1,0:T(8,128)}, u32[]{:S(2)}, u32[]{:S(2)}) collective-permute-start(f32[16,768]{1,0:T(8,128)S(1)} %fusion), channel_id=1, source_target_pairs={{0,112},{8,120},{16,128},{24,136},{32,144},{40,152},{48,160},{56,1... | collective-permute-start | bytes 147464
  240.4 29.8 %collective-permute-start.12 = (f32[16,768]{1,0:T(8,128)S(1)}, f32[16,768]{1,0:T(8,128)}, u32[]{:S(2)}, u32[]{:S(2)}) collective-permute-start(f32[16,768]{1,0:T(8,128)S(1)} %fusion), channel_id=1, source_target_pairs={{0,104},{8,112},{16,120},{24,128},{32,136},{40,144},{48,152},{56,1... | collective-permute-start | bytes 147464
  242.3 38.5 %collective-permute-start.11 = (f32[16,768]{1,0:T(8,128)S(1)}, f32[16,768]{1,0:T(8,128)}, u32[]{:S(2)}, u32[]{:S(2)}) collective-permute-start(f32[16,768]{1,0:T(8,128)S(1)} %fusion), channel_id=1, source_target_pairs={{0,96},{8,104},{16,112},{24,120},{32,128},{40,136},{48,144},{56,15... | collective-permute-start | bytes 147464
  244.8 8.7 %collective-permute-start.15 = (f32[12,768]{1,0:T(8,128)}, f32[12,768]{1,0:T(8,128)}, u32[]{:S(2)}, u32[]{:S(2)}) collective-permute-start(f32[12,768]{1,0:T(8,128)} %slice.240), channel_id=1, source_target_pairs={{0,128},{8,136},{16,144},{24,152},{32,160},{40,168},{48,176},{56,1... | collective-permute-start | bytes 110600
  253.5 28.5 %collective-permute-start.10 = (f32[16,768]{1,0:T(8,128)S(1)}, f32[16,768]{1,0:T(8,128)S(1)}, u32[]{:S(2)}, u32[]{:S(2)}) collective-permute-start(f32[16,768]{1,0:T(8,128)S(1)} %fusion), channel_id=1, source_target_pairs={{0,88},{8,96},{16,104},{24,112},{32,120},{40,128},{48,136},{56,144... | collective-permute-start | bytes 147464
  254.9 34.5 %collective-permute-start.9 = (f32[16,768]{1,0:T(8,128)S(1)}, f32[16,768]{1,0:T(8,128)S(1)}, u32[]{:S(2)}, u32[]{:S(2)}) collective-permute-start(f32[16,768]{1,0:T(8,128)S(1)} %fusion), channel_id=1, source_target_pairs={{0,80},{8,88},{16,96},{24,104},{32,112},{40,120},{48,128},{56,136}... | collective-permute-start | bytes 147464
  268.3 22.4 %collective-permute-start.8 = (f32[16,768]{1,0:T(8,128)S(1)}, f32[16,768]{1,0:T(8,128)S(1)}, u32[]{:S(2)}, u32[]{:S(2)}) collective-permute-start(f32[16,768]{1,0:T(8,128)S(1)} %fusion), channel_id=1, source_target_pairs={{0,72},{8,80},{16,88},{24,96},{32,104},{40,112},{48,120},{56,128},... | collective-permute-start | bytes 147464
  270.2 26.1 %collective-permute-start.7 = (f32[16,768]{1,0:T(8,128)S(1)}, f32[16,768]{1,0:T(8,128)S(1)}, u32[]{:S(2)}, u32[]{:S(2)}) collective-permute-start(f32[16,768]{1,0:T(8,128)S(1)} %fusion), channel_id=1, source_target_pairs={{0,64},{8,72},{16,80},{24,88},{32,96},{40,104},{48,112},{56,120},{... | collective-permute-start | bytes 147464
  280.8 20.4 %collective-permute-start.6 = (f32[16,768]{1,0:T(8,128)S(1)}, f32[16,768]{1,0:T(8,128)S(1)}, u32[]{:S(2)}, u32[]{:S(2)}) collective-permute-start(f32[16,768]{1,0:T(8,128)S(1)} %fusion), channel_id=1, source_target_pairs={{0,56},{8,64},{16,72},{24,80},{32,88},{40,96},{48,104},{56,112},{6... | collective-permute-start | bytes 147464
  282.1 23.9 %copy-start.24 = (f32[16,768]{1,0:T(8,128)}, f32[16,768]{1,0:T(8,128)S(1)}, u32[]{:S(2)}) copy-start(f32[16,768]{1,0:T(8,128)S(1)} %collective-permute-done.10) | copy-start | bytes 147460
  282.1 21.0 %collective-permute-start.5 = (f32[16,768]{1,0:T(8,128)S(1)}, f32[16,768]{1,0:T(8,128)S(1)}, u32[]{:S(2)}, u32[]{:S(2)}) collective-permute-start(f32[16,768]{1,0:T(8,128)S(1)} %fusion), channel_id=1, source_target_pairs={{0,48},{8,56},{16,64},{24,72},{32,80},{40,88},{48,96},{56,104},{64... | collective-permute-start | bytes 147464
  289.4 16.5 %copy-start.25 = (f32[16,768]{1,0:T(8,128)}, f32[16,768]{1,0:T(8,128)S(1)}, u32[]{:S(2)}) copy-start(f32[16,768]{1,0:T(8,128)S(1)} %collective-permute-done.9) | copy-start | bytes 147460
  289.4 18.6 %collective-permute-start.4 = (f32[16,768]{1,0:T(8,128)S(1)}, f32[16,768]{1,0:T(8,128)S(1)}, u32[]{:S(2)}, u32[]{:S(2)}) collective-permute-start(f32[16,768]{1,0:T(8,128)S(1)} %fusion), channel_id=1, source_target_pairs={{0,40},{8,48},{16,56},{24,64},{32,72},{40,80},{48,88},{56,96},{64,... | collective-permute-start | bytes 147464
  290.7 16.6 %copy-start.26 = (f32[16,768]{1,0:T(8,128)}, f32[16,768]{1,0:T(8,128)S(1)}, u32[]{:S(2)}) copy-start(f32[16,768]{1,0:T(8,128)S(1)} %collective-permute-done.8) | copy-start | bytes 147460
  290.7 17.3 %collective-permute-start.3 = (f32[16,768]{1,0:T(8,128)S(1)}, f32[16,768]{1,0:T(8,128)}, u32[]{:S(2)}, u32[]{:S(2)}) collective-permute-start(f32[16,768]{1,0:T(8,128)S(1)} %fusion), channel_id=1, source_target_pairs={{0,32},{8,40},{16,48},{24,56},{32,64},{40,72},{48,80},{56,88},{64,... | collective-permute-start | bytes 147464
  296.4 11.0 %copy-start.27 = (f32[16,768]{1,0:T(8,128)}, f32[16,768]{1,0:T(8,128)S(1)}, u32[]{:S(2)}) copy-start(f32[16,768]{1,0:T(8,128)S(1)} %collective-permute-done.7) | copy-start | bytes 147460
  296.4 11.7 %collective-permute-start.2 = (f32[16,768]{1,0:T(8,128)S(1)}, f32[16,768]{1,0:T(8,128)}, u32[]{:S(2)}, u32[]{:S(2)}) collective-permute-start(f32[16,768]{1,0:T(8,128)S(1)} %fusion), channel_id=1, source_target_pairs={{0,24},{8,32},{16,40},{24,48},{32,56},{40,64},{48,72},{56,80},{64,... | collective-permute-start | bytes 147464
  301.2 6.1 %copy-start.28 = (f32[16,768]{1,0:T(8,128)}, f32[16,768]{1,0:T(8,128)S(1)}, u32[]{:S(2)}) copy-start(f32[16,768]{1,0:T(8,128)S(1)} %collective-permute-done.6) | copy-start | bytes 147460
  301.2 6.9 %collective-permute-start.1 = (f32[16,768]{1,0:T(8,128)S(1)}, f32[16,768]{1,0:T(8,128)}, u32[]{:S(2)}, u32[]{:S(2)}) collective-permute-start(f32[16,768]{1,0:T(8,128)S(1)} %fusion), channel_id=1, source_target_pairs={{0,16},{8,24},{16,32},{24,40},{32,48},{40,56},{48,64},{56,72},{64,... | collective-permute-start | bytes 147464
  303.1 4.2 copy-start.29
  303.1 5.0 %collective-permute-start = (f32[16,768]{1,0:T(8,128)S(1)}, f32[16,768]{1,0:T(8,128)}, u32[]{:S(2)}, u32[]{:S(2)}) collective-permute-start(f32[16,768]{1,0:T(8,128)S(1)} %fusion), channel_id=1, source_target_pairs={{0,8},{8,16},{16,24},{24,32},{32,40},{40,48},{48,56},{56,64},{64,7... | collective-permute-start | bytes 147464
  335.0 9.8 %copy-start.13 = (bf16[8,32,2,48]{3,1,2,0:T(8,128)(2,1)S(1)}, bf16[8,32,2,48]{3,1,2,0:T(8,128)(2,1)}, u32[]{:S(2)}) copy-start(bf16[8,32,2,48]{3,1,2,0:T(8,128)(2,1)} %copy-done.12) | copy-start | bytes 147460
  335.0 103.0 %reduce-scatter.10.cloned.1.call-start = ((), (), s32[]{:S(2)}) async-start(), calls=%async_computation.4 | async-start | bytes 2359296 | tf_op jit(solution)/shard_map/reduce_scatter | solution.py:117
  341.0 140.2 %reduce-scatter.8.cloned.1.call-start = ((), (), s32[]{:S(2)}) async-start(), calls=%async_computation.3 | async-start | bytes 2359296 | tf_op jit(solution)/shard_map/reduce_scatter | solution.py:116
  344.0 0.7 copy-start.10
  344.7 6.8 %copy-start.40 = (f32[32,2]{0,1:T(2,128)S(1)}, f32[32,2]{0,1:T(2,128)}, u32[]{:S(2)}) copy-start(f32[32,2]{0,1:T(2,128)} %copy-done.39) | copy-start | bytes 772
  344.7 6.8 %copy-start.38 = (f32[32,2]{0,1:T(2,128)S(1)}, f32[32,2]{0,1:T(2,128)}, u32[]{:S(2)}) copy-start(f32[32,2]{0,1:T(2,128)} %get-tuple-element.10) | copy-start | bytes 772
  344.7 6.8 %copy-start.37 = (f32[32,2]{0,1:T(2,128)S(1)}, f32[32,2]{0,1:T(2,128)}, u32[]{:S(2)}) copy-start(f32[32,2]{0,1:T(2,128)} %get-tuple-element.9) | copy-start | bytes 772
  344.7 6.9 %copy-start.36 = (f32[32,2]{0,1:T(2,128)S(1)}, f32[32,2]{0,1:T(2,128)}, u32[]{:S(2)}) copy-start(f32[32,2]{0,1:T(2,128)} %get-tuple-element.8) | copy-start | bytes 772
  344.7 6.9 %copy-start.35 = (f32[32,2]{0,1:T(2,128)S(1)}, f32[32,2]{0,1:T(2,128)}, u32[]{:S(2)}) copy-start(f32[32,2]{0,1:T(2,128)} %get-tuple-element.7) | copy-start | bytes 772
  344.8 6.9 %copy-start.34 = (f32[32,2]{0,1:T(2,128)S(1)}, f32[32,2]{0,1:T(2,128)}, u32[]{:S(2)}) copy-start(f32[32,2]{0,1:T(2,128)} %get-tuple-element.6) | copy-start | bytes 772
  344.8 6.9 %copy-start.33 = (f32[32,2]{0,1:T(2,128)S(1)}, f32[32,2]{0,1:T(2,128)}, u32[]{:S(2)}) copy-start(f32[32,2]{0,1:T(2,128)} %get-tuple-element.5) | copy-start | bytes 772
  344.8 6.9 %copy-start.32 = (f32[32,2]{0,1:T(2,128)S(1)}, f32[32,2]{0,1:T(2,128)}, u32[]{:S(2)}) copy-start(f32[32,2]{0,1:T(2,128)} %get-tuple-element.4) | copy-start | bytes 772
  344.8 6.9 %copy-start.16 = (f32[8,32,2]{1,2,0:T(2,128)S(1)}, f32[8,32,2]{1,2,0:T(2,128)}, u32[]{:S(2)}) copy-start(f32[8,32,2]{1,2,0:T(2,128)} %copy-done.15) | copy-start | bytes 6148
  344.8 6.9 %copy-start.19 = (f32[8,32,2]{1,2,0:T(2,128)S(1)}, f32[8,32,2]{1,2,0:T(2,128)}, u32[]{:S(2)}) copy-start(f32[8,32,2]{1,2,0:T(2,128)} %copy-done.18) | copy-start | bytes 6148
  352.7 5.0 %copy-start.3 = (bf16[8,256,2,48]{3,1,2,0:T(8,128)(2,1)S(1)}, bf16[8,256,2,48]{3,1,2,0:T(8,128)(2,1)}, u32[]{:S(2)}) copy-start(bf16[8,256,2,48]{3,1,2,0:T(8,128)(2,1)} %copy-done.2) | copy-start | bytes 1179652
  352.7 5.0 %copy-start.11 = (bf16[8,32,2,256]{3,1,2,0:T(8,128)(2,1)S(1)}, bf16[8,32,2,256]{3,1,2,0:T(8,128)(2,1)}, u32[]{:S(2)}) copy-start(bf16[8,32,2,256]{3,1,2,0:T(8,128)(2,1)} %copy-done.10) | copy-start | bytes 786436
  353.5 5.1 %copy-start.31 = (f32[256,16]{0,1:T(8,128)}, f32[256,16]{0,1:T(8,128)S(1)}, u32[]{:S(2)}) copy-start(f32[256,16]{0,1:T(8,128)S(1)} %multiply_select_fusion) | copy-start | bytes 49156
  366.7 4.0 copy-start.8
Sparse Core Ops, SparseCore 0:
  335.1 59.6 reduce-scatter.11
  397.8 40.0 reduce-scatter.9
  441.1 40.1 reduce-scatter.7
where the time goes:
time: 498 us; the launch traced here: 494 us
  blocking collectives  171 us (34%)
  local copies, waits for them, and re-layouts  106 us (21%)
  waiting for transfers between devices  95.6 us (19%)
  starting transfers between devices  61.8 us (12%)
  matrix products  31.4 us (6%)
  between operations  15.5 us (3%)
  other arithmetic  12.9 us (3%)
    unnamed x1, blocking collectives  136 us
    unnamed x17, starting transfers between devices  61.7 us
    unnamed x140, local copies, waits for them, and re-layouts  47.4 us
    reduce_scatter x1, waiting for transfers between devices, on_device(): lax.psum_scatter(dv_all, 'seq', scatter_dimension=1, tiled=True)  41.7 us
    reduce_scatter x1, waiting for transfers between devices, on_device(): lax.psum_scatter(dk_all, 'seq', scatter_dimension=1, tiled=True)  40.3 us
    all_gather x1, blocking collectives, on_device(): lax.all_gather(k_sel, 'seq', axis=1, tiled=True)  20.6 us
    all_gather x1, blocking collectives, on_device(): lax.all_gather(v_sel, 'seq', axis=1, tiled=True)  15 us
    mul x16, local copies, waits for them, and re-layouts, place(): full = eye[None, :, None, :, None] * moved[:, None, :, :, :]  14 us
  transfers between devices with their start and end apart: 19, of which 3 were waited for; matrix products, arithmetic and copies ran while one was open for 12% of the time, Pallas kernels for 0%

commit v1 on v0

v1 whole, which is shorter than its diff:
```python
import functools

import jax
import jax.numpy as jnp
from jax import lax
from jax.experimental import pallas as pl
from jax.experimental.pallas import tpu as pltpu
from jax.sharding import PartitionSpec as P

MESH = pl.DeviceIdType.MESH
NHEAD = 16
DH = 48
D = NHEAD * DH
SEG = 256
SPREAD = 8
CLS = SEG // SPREAD
PAIR = 2 * DH
SLIDES = 4
PAD = 16
BIG = 2.0**20
LOG2E = 1.4426950408889634
SCALE = DH**-0.5
F32 = jnp.float32
BF16 = jnp.bfloat16


def iota(shape, dim):
    return lax.broadcasted_iota(jnp.int32, shape, dim)


def mm(a, b):
    return jnp.dot(a, b, preferred_element_type=F32)


def mm_tn(a, b):
    return lax.dot_general(a, b, (((0,), (0,)), ((), ())), preferred_element_type=F32)


def mm_nt(a, b):
    return lax.dot_general(a, b, (((1,), (1,)), ((), ())), preferred_element_type=F32)


def mask_rows(pos, ends):
    row = iota((PAD, pos.shape[1]), 0)
    starts = [0] + ends[:-1]
    hit = jnp.zeros((PAD, pos.shape[1]), F32)
    for i in range(SLIDES):
        inside = jnp.where((pos >= starts[i]) & (pos < ends[i]), 1.0, 0.0)
        hit = jnp.where(row == i, inside, hit)
    off = jnp.where(row < SLIDES, (hit - 1.0) * BIG, 0.0)
    return hit.astype(BF16), off.astype(BF16)


def forward_head(qt, kt, vt, dot, k_mask, q_mask, ones):
    s = mm_tn(jnp.concatenate([kt, k_mask], 0), jnp.concatenate([qt, q_mask], 0))
    top = jnp.max(s, 0, keepdims=True)
    e = jnp.exp2((s - top) * (SCALE * LOG2E)).astype(BF16)
    ov = mm(jnp.concatenate([vt, ones], 0), e)
    total = ov[DH : DH + 1]
    o = ov[:DH] * (1.0 / total)
    top = top * (SCALE * LOG2E)
    lse = top + jnp.log(total) * LOG2E
    delta = jnp.sum(dot.astype(F32) * o, 0, keepdims=True)
    return e, o, top, lse, delta


def backward_head(qt, kt, vt, dot, e, ones, ratio, delta):
    hi = delta.astype(BF16)
    lo = (delta - hi.astype(F32)).astype(BF16)
    row = iota((PAD, delta.shape[1]), 0)
    less = jnp.where(row == 0, -hi.astype(F32), jnp.where(row == 1, -lo.astype(F32), 0.0))
    dp = mm_tn(jnp.concatenate([vt, ones], 0), jnp.concatenate([dot, less.astype(BF16)], 0))
    g = (e.astype(F32) * dp).astype(BF16)
    dv = mm_nt((dot.astype(F32) * ratio).astype(BF16), e)
    ratio = ratio * SCALE
    dk = mm_nt((qt.astype(F32) * ratio).astype(BF16), g)
    dq = mm(kt, g) * ratio
    return dq, dk, dv


def merge(lse_a, delta_a, lse_b, delta_b):
    top = jnp.maximum(lse_a, lse_b)
    lse = top + jnp.log(jnp.exp2(lse_a - top) + jnp.exp2(lse_b - top)) * LOG2E
    w_a, w_b = jnp.exp2(lse_a - lse), jnp.exp2(lse_b - lse)
    return lse, w_a, w_b, w_a * delta_a + w_b * delta_b


def lane_block(rows):
    return iota((rows, 128), 1) // CLS


def shift(x, blocks):
    blocks = blocks % 4
    return x if blocks == 0 else pltpu.roll(x, blocks * CLS, 1)


def kernel(
    q_ref, k_ref, v_ref, g_ref, w_ref, len_ref,
    dq_ref, dk_ref, dv_ref, dw_ref,
    qt, kt, vt, dot, pog, e_all, ot, sta, att, dqt, dkt, dvt,
    qb, kb, vb, db, eb, ob, sb,
    send1, recv1, send2, recv2, send3, recv3, send4, recv4,
    ssem, rsem,
):
    dp = lax.axis_index("dp")
    me = lax.axis_index("seq")

    barrier = pltpu.get_barrier_semaphore()
    for d in range(1, SPREAD):
        pl.semaphore_signal(
            barrier, inc=1, device_id=(dp, lax.rem(me + d, SPREAD)), device_id_type=MESH
        )

    ends = []
    for i in range(SLIDES):
        ends.append(len_ref[0, i] if i == 0 else ends[-1] + len_ref[0, i])

    def exchange(kind, send, recv):
        copies = []
        for d in range(1, SPREAD):
            other = lax.rem(me + d, SPREAD)
            copies.append(
                pltpu.make_async_remote_copy(
                    src_ref=send.at[other],
                    dst_ref=recv.at[me],
                    send_sem=ssem.at[kind, d],
                    recv_sem=rsem.at[kind, d],
                    device_id=(dp, other),
                    device_id_type=MESH,
                )
            )
        return copies

    def arrive(kind, send, recv):
        for d in range(1, SPREAD):
            source = lax.rem(me + SPREAD - d, SPREAD)
            pltpu.make_async_remote_copy(
                src_ref=send.at[source],
                dst_ref=recv.at[source],
                send_sem=ssem.at[kind, d],
                recv_sem=rsem.at[kind, d],
                device_id=(dp, source),
                device_id_type=MESH,
            ).wait_recv()

    to = iota((SEG, SEG), 0)
    at = iota((SEG, SEG), 1)
    perm = jnp.where(at == to % CLS * SPREAD + to // CLS, 1.0, 0.0).astype(BF16)
    for src, dst in ((q_ref, qt), (k_ref, kt), (v_ref, vt)):
        moved = mm(perm, src[...]).T.astype(BF16)
        dst[...] = moved.reshape(NHEAD, DH, SEG)
    pog[...] = mm(perm, g_ref[...]).astype(BF16)
    dot[...] = mm_nt(w_ref[...], pog[...]).astype(BF16).reshape(NHEAD, DH, SEG)

    block = lane_block(PAIR)
    for j in range(SPREAD):
        tile = pl.ds(j // 4 * 128, 128)
        out = jnp.zeros((PAIR, 128), F32)
        for t, src in enumerate((qt, kt, vt, dot)):
            both = jnp.concatenate([src[j, :, tile], src[j + SPREAD, :, tile]], 0)
            out = jnp.where(block == t, shift(both.astype(F32), t - j), out)
        send1[j] = out.astype(BF16)
    recv1[me] = send1[me]

    pl.semaphore_wait(barrier, SPREAD - 1)
    copies1 = exchange(0, send1, recv1)
    for c in copies1:
        c.start()

    lane = iota((1, SEG), 1)
    k_mask, q_mask = mask_rows(me * SEG + lane % CLS * SPREAD + lane // CLS, ends)
    row = iota((PAD, SEG), 0)
    ones = jnp.where(row < 2, 1.0, 0.0).astype(BF16)

    def forward(h, carry):
        e, o, top, lse, delta = forward_head(
            qt[h], kt[h], vt[h], dot[h], k_mask, q_mask, ones
        )
        e_all[h] = e
        ot[h] = o
        sta[h, 0:1] = top
        sta[h, 1:2] = lse
        sta[h, 2:3] = delta
        return carry

    lax.fori_loop(0, NHEAD, forward, 0)

    narrow = lane_block(8)
    for j in range(SPREAD):
        tile = pl.ds(j // 4 * 128, 128)
        rows = jnp.concatenate(
            [sta[j, 1:2, tile], sta[j + SPREAD, 1:2, tile],
             sta[j, 2:3, tile], sta[j + SPREAD, 2:3, tile],
             jnp.zeros((4, 128), F32)], 0)
        send2[j] = shift(rows, -j)
    recv2[me] = send2[me]
    copies2 = exchange(1, send2, recv2)
    for c in copies2:
        c.start()

    arrive(0, send1, recv1)
    for half in range(2):
        tile = pl.ds(half * 128, 128)
        outs = [jnp.zeros((PAIR, 128), F32)] * 4
        for s in range(half * 4, half * 4 + 4):
            got = recv1[s].astype(F32)
            for t in range(4):
                outs[t] = jnp.where(block == s % 4, shift(got, s - t), outs[t])
        for dst, out in zip((qb, kb, vb, db), outs):
            out = out.astype(BF16)
            for u in range(2):
                dst[u, :, tile] = out[u * DH : (u + 1) * DH]
    kb_mask, qb_mask = mask_rows(lane * SPREAD + me, ends)
    for u in range(2):
        e, o, top, lse, delta = forward_head(
            qb[u], kb[u], vb[u], db[u], kb_mask, qb_mask, ones
        )
        eb[u] = e
        ob[u] = o
        sb[u, 0:1] = top
        sb[u, 1:2] = lse
        sb[u, 2:3] = delta

    wide = lane_block(CLS)
    for s in range(SPREAD):
        tile = pl.ds(s // 4 * 128, 128)
        rows = jnp.concatenate(
            [sb[0, 1:2, tile], sb[1, 1:2, tile], sb[0, 2:3, tile], sb[1, 2:3, tile],
             jnp.zeros((4, 128), F32)], 0)
        both = jnp.concatenate([ob[0, :, tile], ob[1, :, tile]], 0)
        out = jnp.zeros((CLS, 128), F32)
        for g in range(3):
            out = jnp.where(wide == g, shift(both[g * CLS : (g + 1) * CLS], g - s), out)
        stat = jnp.concatenate([shift(rows, 3 - s), jnp.zeros((CLS - 8, 128), F32)], 0)
        send3[s] = jnp.where(wide == 3, stat, out)
    recv3[me] = send3[me]
    copies3 = exchange(2, send3, recv3)
    for c in copies3:
        c.start()

    arrive(1, send2, recv2)
    halves = []
    for half in range(2):
        out = jnp.zeros((8, 128), F32)
        for s in range(half * 4, half * 4 + 4):
            out = jnp.where(narrow == s % 4, shift(recv2[s], s), out)
        halves.append(out)
    theirs = jnp.concatenate(halves, 1)
    for u in range(2):
        top = sb[u, 0:1]
        lse, _, _, delta = merge(theirs[u : u + 1], theirs[2 + u : 3 + u], sb[u, 1:2], sb[u, 2:3])
        dq, dk, dv = backward_head(
            qb[u], kb[u], vb[u], db[u], eb[u], ones, jnp.exp2(top - lse), delta
        )
        for s in range(SPREAD):
            tile = slice(s // 4 * 128, s // 4 * 128 + 128)
            out = jnp.zeros((DH, 128), F32)
            for t, x in enumerate((dq, dk, dv)):
                out = jnp.where(lane_block(DH) == t, shift(x[:, tile], t - s), out)
            send4[s, u * DH : (u + 1) * DH] = out.astype(BF16)
    recv4[me] = send4[me]
    copies4 = exchange(3, send4, recv4)
    for c in copies4:
        c.start()

    arrive(2, send3, recv3)
    tall = iota((NHEAD, 128), 0)
    spot = lane_block(NHEAD)
    lse_b, delta_b = [], []
    for half in range(2):
        lb = jnp.full((NHEAD, 128), -1e30, F32)
        dbl = jnp.zeros((NHEAD, 128), F32)
        for j in range(half * 4, half * 4 + 4):
            x = shift(recv3[j, 0:8], j - 3)
            for u in range(2):
                here = (tall == j + SPREAD * u) & (spot == j % 4)
                lb = jnp.where(here, x[u : u + 1], lb)
                dbl = jnp.where(here, x[2 + u : 3 + u], dbl)
        lse_b.append(lb)
        delta_b.append(dbl)
    lse_b, delta_b = jnp.concatenate(lse_b, 1), jnp.concatenate(delta_b, 1)
    lse, w_a, w_b, delta = merge(sta[:, 1, :], sta[:, 2, :], lse_b, delta_b)
    sta[:, 2, :] = delta
    sta[:, 3, :] = jnp.exp2(sta[:, 0, :] - lse)
    for j in range(SPREAD):
        got = recv3[j]
        other = jnp.concatenate([shift(got, j - g) for g in range(3)], 0)
        for u in range(2):
            h = j + SPREAD * u
            for half in range(2):
                tile = slice(half * 128, half * 128 + 128)
                x = ot[h, :, tile] * w_a[h : h + 1, tile]
                if half == j // 4:
                    part = other[u * DH : (u + 1) * DH] * w_b[h : h + 1, tile]
                    x = x + jnp.where(lane_block(DH) == j % 4, part, 0.0)
                att[h * DH : (h + 1) * DH, tile] = x.astype(BF16)
    dw_ref[...] = mm(att[...], pog[...])

    def backward(h, carry):
        dq, dk, dv = backward_head(
            qt[h], kt[h], vt[h], dot[h], e_all[h], ones, sta[h, 3:4], sta[h, 2:3]
        )
        dqt[h] = dq
        dkt[h] = dk
        dvt[h] = dv
        return carry

    lax.fori_loop(0, NHEAD, backward, 0)

    arrive(3, send4, recv4)
    for j in range(SPREAD):
        tile = pl.ds(j // 4 * 128, 128)
        got = recv4[j].astype(F32)
        for t, dst in enumerate((dqt, dkt, dvt)):
            part = jnp.where(block == j % 4, shift(got, j - t), 0.0)
            for u in range(2):
                h = j + SPREAD * u
                dst[h, :, tile] = dst[h, :, tile] + part[u * DH : (u + 1) * DH]
    back = jnp.where(to == at % CLS * SPREAD + at // CLS, 1.0, 0.0).astype(BF16)
    for src, dst in ((dqt, dq_ref), (dkt, dk_ref), (dvt, dv_ref)):
        dst[...] = mm_nt(back, src[...].reshape(D, SEG).astype(BF16)).astype(BF16)

    for c in copies1 + copies2 + copies3 + copies4:
        c.wait_send()


def on_device(queries, keys, values, out_grad, out_weight, slide_lengths):
    vmem = pl.BlockSpec(memory_space=pltpu.VMEM)
    heads = lambda n, dtype: pltpu.VMEM((n, DH, SEG), dtype)
    dq, dk, dv, partial = pl.pallas_call(
        kernel,
        out_shape=(
            jax.ShapeDtypeStruct((SEG, D), BF16),
            jax.ShapeDtypeStruct((SEG, D), BF16),
            jax.ShapeDtypeStruct((SEG, D), BF16),
            jax.ShapeDtypeStruct((D, D), F32),
        ),
        in_specs=[vmem] * 5 + [pl.BlockSpec(memory_space=pltpu.SMEM)],
        out_specs=(vmem,) * 4,
        scratch_shapes=[
            heads(NHEAD, BF16), heads(NHEAD, BF16), heads(NHEAD, BF16), heads(NHEAD, BF16),
            pltpu.VMEM((SEG, D), BF16),
            pltpu.VMEM((NHEAD, SEG, SEG), BF16),
            heads(NHEAD, F32),
            pltpu.VMEM((NHEAD, 8, SEG), F32),
            pltpu.VMEM((D, SEG), BF16),
            heads(NHEAD, F32), heads(NHEAD, F32), heads(NHEAD, F32),
            heads(2, BF16), heads(2, BF16), heads(2, BF16), heads(2, BF16),
            pltpu.VMEM((2, SEG, SEG), BF16),
            heads(2, F32),
            pltpu.VMEM((2, 8, SEG), F32),
            pltpu.VMEM((SPREAD, PAIR, 128), BF16), pltpu.VMEM((SPREAD, PAIR, 128), BF16),
            pltpu.VMEM((SPREAD, 8, 128), F32), pltpu.VMEM((SPREAD, 8, 128), F32),
            pltpu.VMEM((SPREAD, CLS, 128), F32), pltpu.VMEM((SPREAD, CLS, 128), F32),
            pltpu.VMEM((SPREAD, PAIR, 128), BF16), pltpu.VMEM((SPREAD, PAIR, 128), BF16),
            pltpu.SemaphoreType.DMA((4, SPREAD)),
            pltpu.SemaphoreType.DMA((4, SPREAD)),
        ],
        compiler_params=pltpu.CompilerParams(
            collective_id=0, has_side_effects=True, vmem_limit_bytes=48 * 1024 * 1024
        ),
    )(queries, keys, values, out_grad, out_weight, slide_lengths)
    rows_mine = lax.psum_scatter(partial, "dp", scatter_dimension=0, tiled=True)
    weight_grad = lax.psum_scatter(rows_mine, "seq", scatter_dimension=1, tiled=True)
    return dq, dk, dv, weight_grad


def solution(mesh):
    placed = (
        P(("dp", "seq"), None),
        P(("dp", "seq"), None),
        P(("dp", "seq"), None),
        P(("dp", "seq"), None),
        P(),
        P("dp", None),
    )
    return jax.shard_map(
        on_device,
        mesh=mesh,
        in_specs=placed,
        out_specs=(
            P(("dp", "seq"), None),
            P(("dp", "seq"), None),
            P(("dp", "seq"), None),
            P("dp", "seq"),
        ),
        check_vma=False,
    )
```

time: 498 us -> 331 us (0.66)
  local copies, waits for them, and re-layouts: 106 us -> 13.9 us
  blocking collectives: 171 us -> 136 us
  matrix products: 31.4 us -> 0 us
  Pallas kernels: 0 us -> 30.8 us
  waiting for transfers between devices: 95.6 us -> 70.8 us
  other arithmetic: 12.9 us -> 0 us
    reduce_scatter x2 -> x0, waiting for transfers between devices: 82.1 us -> none  [the longest x1 41.7 us: on_device(): lax.psum_scatter(dv_all, 'seq', scatter_dimension=1, tiled=True)]
    unnamed x20 -> x18, waiting for transfers between devices: 13.5 us -> 70.8 us
    all_gather x2 -> x0, blocking collectives: 35.6 us -> none  [the longest x1 20.6 us: on_device(): lax.all_gather(k_sel, 'seq', axis=1, tiled=True)]
    unnamed x140 -> x21, local copies, waits for them, and re-layouts: 47.4 us -> 13.9 us
    dot_general x14 -> x0, matrix products: 31.4 us -> none  [the longest x2 6.51 us: attend_backward(): jnp.einsum('cqhk,cqhd->ckhd', prob.astype(jnp.bfloat16), dout, preferred_...]
    pallas_call x0 -> x1, Pallas kernels: none -> 30.8 us  [on_device(): pl.pallas_call(kernel, out_shape=(jax.ShapeDtypeStruct((SEG, D), BF16), j...]
    mul x16 -> x0, local copies, waits for them, and re-layouts: 14 us -> none  [place(): full = eye[None, :, None, :, None] * moved[:, None, :, :, :]]
    another operation x11 -> x0, local copies, waits for them, and re-layouts: 12.6 us -> none  [the longest x4 11.3 us: pick(): array.reshape(count // spread, spread, heads // spread, spread, inner)]
  transfers between devices with their start and end apart: 19 -> 17, of which waited for: 3 -> 1; matrix products, arithmetic and copies ran while one was open for 12% -> 0% of each run, Pallas kernels for 0% -> 0%
where the time goes in v1:
time: 331 us; the launch traced here: 330 us
  blocking collectives  136 us (41%)
  waiting for transfers between devices  70.8 us (21%)
  starting transfers between devices  63.4 us (19%)
  Pallas kernels  30.8 us (9%)
  between operations  15 us (5%)
  local copies, waits for them, and re-layouts  13.9 us (4%)
    unnamed x1, blocking collectives  136 us
    unnamed x18, waiting for transfers between devices  70.8 us
    unnamed x17, starting transfers between devices  63.4 us
    pallas_call x1, Pallas kernels, on_device(): pl.pallas_call(kernel, out_shape=(jax.ShapeDtypeStruct((SEG, D), BF16), j...  30.8 us
    unnamed x21, local copies, waits for them, and re-layouts  13.9 us
  transfers between devices with their start and end apart: 17, of which 1 were waited for; matrix products, arithmetic and copies ran while one was open for 0% of the time, Pallas kernels for 0%

profile of v1, /device:TPU:1, one launch (start us, length us, event | category | flops | bytes accessed | tf_op | source)
XLA Modules:
  0.0 329.8 jit_solution(15272753054684615033)
XLA Ops:
  7.2 0.0 reduce-scatter.6.cloned.1.call-start
  7.2 0.0 copy-start
  7.2 1.3 copy-done
  8.5 0.0 copy-start.1
  8.5 1.0 copy-done.1
  9.5 0.0 copy-start.2
  9.5 1.0 copy-done.2
  10.5 0.0 copy-start.3
  10.5 1.0 copy-done.3
  11.5 0.0 copy-start.4
  11.5 1.0 copy-done.4
  12.5 0.0 copy-start.5
  12.5 0.7 copy-done.5
  13.1 30.8 %shard_map.93 = (bf16[256,768]{1,0:T(8,128)(2,1)S(1)}, bf16[256,768]{1,0:T(8,128)(2,1)S(1)}, bf16[256,768]{1,0:T(8,128)(2,1)S(1)}, f32[768,768]{1,0:T(8,128)}) custom-call(bf16[256,768]{1,0:T(8,128)(2,1)S(1)} %copy-done.1, bf16[256,768]{1,0:T(8,128)(2,1)S(1)} %copy-done.2, bf16[256,768]{1,0:T(8,128)(2,1)S(1)} %copy-done.3, bf16[256,768]{1,0:T(8,128)(2,1)S(1)} %copy-done.4, ...), custom_call_target="tpu_custom_call" | custom-call | tf_op jit(solution)/shard_map/pallas_call | solution.py:330
  44.0 135.9 %fusion = f32[16,768]{1,0:T(8,128)S(1)} fusion(f32[768,768]{1,0:T(8,128)} %get-tuple-element.11), kind=kCustom, calls=%all-reduce-scatter | all-reduce-scatter fusion | flops 786433 | bytes 2410496
  179.9 1.3 collective-permute-start.15
  181.2 1.3 collective-permute-start
  182.5 1.3 collective-permute-start.1
  183.8 1.3 collective-permute-start.10
  185.1 1.3 collective-permute-start.11
  186.4 0.0 collective-permute-done.15
  186.4 1.9 collective-permute-start.12
  188.3 0.0 collective-permute-done
  188.3 4.9 %collective-permute-start.13 = (f32[16,768]{1,0:T(8,128)S(1)}, f32[16,768]{1,0:T(8,128)S(1)}, u32[]{:S(2)}, u32[]{:S(2)}) collective-permute-start(f32[16,768]{1,0:T(8,128)S(1)} %fusion), channel_id=1, source_target_pairs={{0,112},{8,120},{16,128},{24,136},{32,144},{40,152},{48,160},{56,1... | collective-permute-start | bytes 147464
  193.3 0.0 collective-permute-done.1
  193.3 4.9 %collective-permute-start.14 = (f32[16,768]{1,0:T(8,128)S(1)}, f32[16,768]{1,0:T(8,128)S(1)}, u32[]{:S(2)}, u32[]{:S(2)}) collective-permute-start(f32[16,768]{1,0:T(8,128)S(1)} %fusion), channel_id=1, source_target_pairs={{0,120},{8,128},{16,136},{24,144},{32,152},{40,160},{48,168},{56,1... | collective-permute-start | bytes 147464
  198.2 0.0 collective-permute-done.10
  198.2 6.1 %collective-permute-start.2 = (f32[16,768]{1,0:T(8,128)S(1)}, f32[16,768]{1,0:T(8,128)S(1)}, u32[]{:S(2)}, u32[]{:S(2)}) collective-permute-start(f32[16,768]{1,0:T(8,128)S(1)} %fusion), channel_id=1, source_target_pairs={{0,24},{8,32},{16,40},{24,48},{32,56},{40,64},{48,72},{56,80},{64,... | collective-permute-start | bytes 147464
  204.3 0.0 collective-permute-done.11
  204.3 6.4 %collective-permute-start.3 = (f32[16,768]{1,0:T(8,128)S(1)}, f32[16,768]{1,0:T(8,128)S(1)}, u32[]{:S(2)}, u32[]{:S(2)}) collective-permute-start(f32[16,768]{1,0:T(8,128)S(1)} %fusion), channel_id=1, source_target_pairs={{0,32},{8,40},{16,48},{24,56},{32,64},{40,72},{48,80},{56,88},{64,... | collective-permute-start | bytes 147464
  210.7 0.0 collective-permute-done.12
  210.7 5.8 %collective-permute-start.4 = (f32[16,768]{1,0:T(8,128)S(1)}, f32[16,768]{1,0:T(8,128)S(1)}, u32[]{:S(2)}, u32[]{:S(2)}) collective-permute-start(f32[16,768]{1,0:T(8,128)S(1)} %fusion), channel_id=1, source_target_pairs={{0,40},{8,48},{16,56},{24,64},{32,72},{40,80},{48,88},{56,96},{64,... | collective-permute-start | bytes 147464
  216.5 0.0 collective-permute-done.13
  216.5 2.9 collective-permute-start.5
  219.4 0.0 collective-permute-done.14
  219.4 8.5 %collective-permute-start.6 = (f32[16,768]{1,0:T(8,128)S(1)}, f32[16,768]{1,0:T(8,128)S(1)}, u32[]{:S(2)}, u32[]{:S(2)}) collective-permute-start(f32[16,768]{1,0:T(8,128)S(1)} %fusion), channel_id=1, source_target_pairs={{0,56},{8,64},{16,72},{24,80},{32,88},{40,96},{48,104},{56,112},{6... | collective-permute-start | bytes 147464
  227.9 0.0 collective-permute-done.2
  227.9 4.3 %collective-permute-start.7 = (f32[16,768]{1,0:T(8,128)S(1)}, f32[16,768]{1,0:T(8,128)S(1)}, u32[]{:S(2)}, u32[]{:S(2)}) collective-permute-start(f32[16,768]{1,0:T(8,128)S(1)} %fusion), channel_id=1, source_target_pairs={{0,64},{8,72},{16,80},{24,88},{32,96},{40,104},{48,112},{56,120},{... | collective-permute-start | bytes 147464
  232.3 0.0 collective-permute-done.3
  232.3 5.2 %collective-permute-start.8 = (f32[16,768]{1,0:T(8,128)S(1)}, f32[16,768]{1,0:T(8,128)S(1)}, u32[]{:S(2)}, u32[]{:S(2)}) collective-permute-start(f32[16,768]{1,0:T(8,128)S(1)} %fusion), channel_id=1, source_target_pairs={{0,72},{8,80},{16,88},{24,96},{32,104},{40,112},{48,120},{56,128},... | collective-permute-start | bytes 147464
  237.5 0.0 collective-permute-done.4
  237.5 6.0 %collective-permute-start.9 = (f32[16,768]{1,0:T(8,128)S(1)}, f32[16,768]{1,0:T(8,128)S(1)}, u32[]{:S(2)}, u32[]{:S(2)}) collective-permute-start(f32[16,768]{1,0:T(8,128)S(1)} %fusion), channel_id=1, source_target_pairs={{0,80},{8,88},{16,96},{24,104},{32,112},{40,120},{48,128},{56,136}... | collective-permute-start | bytes 147464
  243.5 1.3 dynamic-slice.4
  245.4 0.0 collective-permute-done.5
  245.4 0.0 collective-permute-done.6
  245.5 0.0 collective-permute-done.7
  245.5 0.0 collective-permute-done.8
  245.5 0.0 collective-permute-done.9
  245.5 2.1 concatenate
  247.6 0.9 copy.10
  248.5 0.0 reduce-scatter.6.cloned.1.call-update
  248.5 70.7 %reduce-scatter.6.cloned.1.call-done = f32[96,12]{1,0:T(8,128)} async-done(((f32[768,12]{1,0:T(8,128)}), f32[96,12]{1,0:T(8,128)}) %reduce-scatter.6.cloned.1.call-update) | async-done | bytes 4624
  319.2 1.5 copy.11
  320.7 0.7 copy.15
  321.5 0.7 copy.16
  322.2 0.7 copy.17
  (2 shorter events, 0.0 us)
Async XLA Ops:
  7.2 312.1 %reduce-scatter.6.cloned.1.call-start = ((), (), s32[]{:S(2)}) async-start(), calls=%async_computation.1 | async-start | bytes 442368
  7.2 1.3 copy-start
  8.5 1.0 copy-start.1
  9.5 1.0 copy-start.2
  10.5 1.0 copy-start.3
  11.5 1.0 copy-start.4
  12.5 0.7 copy-start.5
  179.9 6.5 %collective-permute-start.15 = (f32[12,768]{1,0:T(8,128)S(1)}, f32[12,768]{1,0:T(8,128)S(1)}, u32[]{:S(2)}, u32[]{:S(2)}) collective-permute-start(f32[12,768]{1,0:T(8,128)S(1)} %slice), channel_id=1, source_target_pairs={{0,128},{8,136},{16,144},{24,152},{32,160},{40,168},{48,176},{56,1... | collective-permute-start | bytes 110600
  181.2 7.1 %collective-permute-start = (f32[16,768]{1,0:T(8,128)S(1)}, f32[16,768]{1,0:T(8,128)S(1)}, u32[]{:S(2)}, u32[]{:S(2)}) collective-permute-start(f32[16,768]{1,0:T(8,128)S(1)} %fusion), channel_id=1, source_target_pairs={{0,8},{8,16},{16,24},{24,32},{32,40},{40,48},{48,56},{56,64},{64,7... | collective-permute-start | bytes 147464
  182.5 10.7 %collective-permute-start.1 = (f32[16,768]{1,0:T(8,128)S(1)}, f32[16,768]{1,0:T(8,128)S(1)}, u32[]{:S(2)}, u32[]{:S(2)}) collective-permute-start(f32[16,768]{1,0:T(8,128)S(1)} %fusion), channel_id=1, source_target_pairs={{0,16},{8,24},{16,32},{24,40},{32,48},{40,56},{48,64},{56,72},{64,... | collective-permute-start | bytes 147464
  183.8 14.4 %collective-permute-start.10 = (f32[16,768]{1,0:T(8,128)S(1)}, f32[16,768]{1,0:T(8,128)S(1)}, u32[]{:S(2)}, u32[]{:S(2)}) collective-permute-start(f32[16,768]{1,0:T(8,128)S(1)} %fusion), channel_id=1, source_target_pairs={{0,88},{8,96},{16,104},{24,112},{32,120},{40,128},{48,136},{56,144... | collective-permute-start | bytes 147464
  185.1 19.2 %collective-permute-start.11 = (f32[16,768]{1,0:T(8,128)S(1)}, f32[16,768]{1,0:T(8,128)S(1)}, u32[]{:S(2)}, u32[]{:S(2)}) collective-permute-start(f32[16,768]{1,0:T(8,128)S(1)} %fusion), channel_id=1, source_target_pairs={{0,96},{8,104},{16,112},{24,120},{32,128},{40,136},{48,144},{56,15... | collective-permute-start | bytes 147464
  186.4 24.3 %collective-permute-start.12 = (f32[16,768]{1,0:T(8,128)S(1)}, f32[16,768]{1,0:T(8,128)S(1)}, u32[]{:S(2)}, u32[]{:S(2)}) collective-permute-start(f32[16,768]{1,0:T(8,128)S(1)} %fusion), channel_id=1, source_target_pairs={{0,104},{8,112},{16,120},{24,128},{32,136},{40,144},{48,152},{56,1... | collective-permute-start | bytes 147464
  188.3 28.2 %collective-permute-start.13 = (f32[16,768]{1,0:T(8,128)S(1)}, f32[16,768]{1,0:T(8,128)S(1)}, u32[]{:S(2)}, u32[]{:S(2)}) collective-permute-start(f32[16,768]{1,0:T(8,128)S(1)} %fusion), channel_id=1, source_target_pairs={{0,112},{8,120},{16,128},{24,136},{32,144},{40,152},{48,160},{56,1... | collective-permute-start | bytes 147464
  193.3 26.1 %collective-permute-start.14 = (f32[16,768]{1,0:T(8,128)S(1)}, f32[16,768]{1,0:T(8,128)S(1)}, u32[]{:S(2)}, u32[]{:S(2)}) collective-permute-start(f32[16,768]{1,0:T(8,128)S(1)} %fusion), channel_id=1, source_target_pairs={{0,120},{8,128},{16,136},{24,144},{32,152},{40,160},{48,168},{56,1... | collective-permute-start | bytes 147464
  198.2 29.7 %collective-permute-start.2 = (f32[16,768]{1,0:T(8,128)S(1)}, f32[16,768]{1,0:T(8,128)S(1)}, u32[]{:S(2)}, u32[]{:S(2)}) collective-permute-start(f32[16,768]{1,0:T(8,128)S(1)} %fusion), channel_id=1, source_target_pairs={{0,24},{8,32},{16,40},{24,48},{32,56},{40,64},{48,72},{56,80},{64,... | collective-permute-start | bytes 147464
  204.3 27.9 %collective-permute-start.3 = (f32[16,768]{1,0:T(8,128)S(1)}, f32[16,768]{1,0:T(8,128)S(1)}, u32[]{:S(2)}, u32[]{:S(2)}) collective-permute-start(f32[16,768]{1,0:T(8,128)S(1)} %fusion), channel_id=1, source_target_pairs={{0,32},{8,40},{16,48},{24,56},{32,64},{40,72},{48,80},{56,88},{64,... | collective-permute-start | bytes 147464
  210.7 26.8 %collective-permute-start.4 = (f32[16,768]{1,0:T(8,128)S(1)}, f32[16,768]{1,0:T(8,128)S(1)}, u32[]{:S(2)}, u32[]{:S(2)}) collective-permute-start(f32[16,768]{1,0:T(8,128)S(1)} %fusion), channel_id=1, source_target_pairs={{0,40},{8,48},{16,56},{24,64},{32,72},{40,80},{48,88},{56,96},{64,... | collective-permute-start | bytes 147464
  216.5 28.9 %collective-permute-start.5 = (f32[16,768]{1,0:T(8,128)S(1)}, f32[16,768]{1,0:T(8,128)S(1)}, u32[]{:S(2)}, u32[]{:S(2)}) collective-permute-start(f32[16,768]{1,0:T(8,128)S(1)} %fusion), channel_id=1, source_target_pairs={{0,48},{8,56},{16,64},{24,72},{32,80},{40,88},{48,96},{56,104},{64... | collective-permute-start | bytes 147464
  219.4 26.0 %collective-permute-start.6 = (f32[16,768]{1,0:T(8,128)S(1)}, f32[16,768]{1,0:T(8,128)S(1)}, u32[]{:S(2)}, u32[]{:S(2)}) collective-permute-start(f32[16,768]{1,0:T(8,128)S(1)} %fusion), channel_id=1, source_target_pairs={{0,56},{8,64},{16,72},{24,80},{32,88},{40,96},{48,104},{56,112},{6... | collective-permute-start | bytes 147464
  227.9 17.6 %collective-permute-start.7 = (f32[16,768]{1,0:T(8,128)S(1)}, f32[16,768]{1,0:T(8,128)S(1)}, u32[]{:S(2)}, u32[]{:S(2)}) collective-permute-start(f32[16,768]{1,0:T(8,128)S(1)} %fusion), channel_id=1, source_target_pairs={{0,64},{8,72},{16,80},{24,88},{32,96},{40,104},{48,112},{56,120},{... | collective-permute-start | bytes 147464
  232.3 13.2 %collective-permute-start.8 = (f32[16,768]{1,0:T(8,128)S(1)}, f32[16,768]{1,0:T(8,128)S(1)}, u32[]{:S(2)}, u32[]{:S(2)}) collective-permute-start(f32[16,768]{1,0:T(8,128)S(1)} %fusion), channel_id=1, source_target_pairs={{0,72},{8,80},{16,88},{24,96},{32,104},{40,112},{48,120},{56,128},... | collective-permute-start | bytes 147464
  237.5 8.0 %collective-permute-start.9 = (f32[16,768]{1,0:T(8,128)S(1)}, f32[16,768]{1,0:T(8,128)S(1)}, u32[]{:S(2)}, u32[]{:S(2)}) collective-permute-start(f32[16,768]{1,0:T(8,128)S(1)} %fusion), channel_id=1, source_target_pairs={{0,80},{8,88},{16,96},{24,104},{32,112},{40,120},{48,128},{56,136}... | collective-permute-start | bytes 147464
Sparse Core Ops, SparseCore 0:
  248.7 70.5 reduce-scatter.5

commit v2 on v1

--- a/solution.py
+++ b/solution.py
@@ -16,6 +16,11 @@
 CLS = SEG // SPREAD
 PAIR = 2 * DH
 SLIDES = 4
+NX = 4
+NY = 4
+NZ = 16
+COLS = D // SPREAD
+COLH = D // 2
 PAD = 16
 BIG = 2.0**20
 LOG2E = 1.4426950408889634
@@ -89,26 +94,60 @@
     return iota((rows, 128), 1) // CLS
 
 
+def pick_rows(count, step, width, padded):
+    r = iota((count * padded, width), 0)
+    at = iota((count * padded, width), 1)
+    inside = (r % padded < step) & (at == r // padded * step + r % padded)
+    return jnp.where(inside, 1.0, 0.0).astype(BF16)
+
+
+def up(n, to):
+    return (n + to - 1) // to * to
+
+
 def shift(x, blocks):
     blocks = blocks % 4
     return x if blocks == 0 else pltpu.roll(x, blocks * CLS, 1)
 
 
 def kernel(
-    q_ref, k_ref, v_ref, g_ref, w_ref, len_ref,
+    q_in, k_in, v_in, g_in, w_in, len_ref,
     dq_ref, dk_ref, dv_ref, dw_ref,
+    q_ref, k_ref, v_ref, g_ref, w_ref, isem,
     qt, kt, vt, dot, pog, e_all, ot, sta, att, dqt, dkt, dvt,
     qb, kb, vb, db, eb, ob, sb,
     send1, recv1, send2, recv2, send3, recv3, send4, recv4,
     ssem, rsem,
+    ogt, c_send, c_recv, a1_send, a1_recv, a2_send, a2_recv, b1_send, b1_recv, b2_send, b2_recv,
+    z_send, z_recv, c_sem, a1_sem, a2_sem, b1_sem, b2_sem, z_sem,
 ):
     dp = lax.axis_index("dp")
     me = lax.axis_index("seq")
+    my, mz, mx, mc = dp // NZ, dp % NZ, me // 2, me % 2
+    half_rows = D // NY // 2
+    wide_rows = up(half_rows, 128)
+    z_rows = D // (NY * NZ)
+    z_pad = up(z_rows, 16)
+
+    loads = []
+    for i, (src, dst) in enumerate(
+        ((q_in, q_ref), (k_in, k_ref), (v_in, v_ref), (g_in, g_ref), (w_in, w_ref))
+    ):
+        loads.append(pltpu.make_async_copy(src, dst, isem.at[i]))
+        loads[-1].start()
 
     barrier = pltpu.get_barrier_semaphore()
     for d in range(1, SPREAD):
         pl.semaphore_signal(
             barrier, inc=1, device_id=(dp, lax.rem(me + d, SPREAD)), device_id_type=MESH
+        )
+    for d in range(1, NY):
+        pl.semaphore_signal(
+            barrier, inc=1, device_id=(lax.rem(my + d, NY) * NZ + mz, me), device_id_type=MESH
+        )
+    for d in range(1, NZ):
+        pl.semaphore_signal(
+            barrier, inc=1, device_id=(my * NZ + lax.rem(mz + d, NZ), me), device_id_type=MESH
         )
 
     ends = []
@@ -143,12 +182,89 @@
                 device_id_type=MESH,
             ).wait_recv()
 
+    def along(size, place, device, send, recv, sem):
+        def copy(d, slot, other):
+            return pltpu.make_async_remote_copy(
+                src_ref=send.at[other],
+                dst_ref=recv.at[slot],
+                send_sem=sem.at[0, d],
+                recv_sem=sem.at[1, d],
+                device_id=device(other),
+                device_id_type=MESH,
+            )
+
+        def start():
+            recv[place] = send[place]
+            for d in range(1, size):
+                copy(d, place, lax.rem(place + d, size)).start()
+
+        def finish():
+            for d in range(1, size):
+                source = lax.rem(place + size - d, size)
+                copy(d, source, source).wait_recv()
+
+        def sent():
+            for d in range(1, size):
+                copy(d, place, lax.rem(place + d, size)).wait_send()
+
+        return start, finish, sent
+
+    def across(send, recv, sem):
+        def copy(b, slot, other):
+            return pltpu.make_async_remote_copy(
+                src_ref=send.at[b],
+                dst_ref=recv.at[slot],
+                send_sem=sem.at[0, b],
+                recv_sem=sem.at[1, slot],
+                device_id=(dp, other),
+                device_id_type=MESH,
+            )
+
+        def start():
+            for b in range(NX):
+                other = 4 * mc + b
+
+                @pl.when(other != me)
+                def _():
+                    copy(b, mx, other).start()
+
+                @pl.when(other == me)
+                def _():
+                    recv[mx] = send[b]
+
+        def finish():
+            for x in range(NX):
+                source = 2 * x + me // 4
+
+                @pl.when(source != me)
+                def _():
+                    copy(0, x, source).wait_recv()
+
+        def sent():
+            for b in range(NX):
+                other = 4 * mc + b
+
+                @pl.when(other != me)
+                def _():
+                    copy(b, mx, other).wait_send()
+
+        return start, finish, sent
+
+    def total(recv, count):
+        out = recv[0].astype(F32)
+        for i in range(1, count):
+            out = out + recv[i].astype(F32)
+        return out
+
     to = iota((SEG, SEG), 0)
     at = iota((SEG, SEG), 1)
     perm = jnp.where(at == to % CLS * SPREAD + to // CLS, 1.0, 0.0).astype(BF16)
-    for src, dst in ((q_ref, qt), (k_ref, kt), (v_ref, vt)):
+    for i, (src, dst) in enumerate(((q_ref, qt), (k_ref, kt), (v_ref, vt))):
+        loads[i].wait()
         moved = mm(perm, src[...]).T.astype(BF16)
         dst[...] = moved.reshape(NHEAD, DH, SEG)
+    loads[3].wait()
+    loads[4].wait()
     pog[...] = mm(perm, g_ref[...]).astype(BF16)
     dot[...] = mm_nt(w_ref[...], pog[...]).astype(BF16).reshape(NHEAD, DH, SEG)
 
@@ -162,7 +278,7 @@
         send1[j] = out.astype(BF16)
     recv1[me] = send1[me]
 
-    pl.semaphore_wait(barrier, SPREAD - 1)
+    pl.semaphore_wait(barrier, SPREAD - 1 + NY - 1 + NZ - 1)
     copies1 = exchange(0, send1, recv1)
     for c in copies1:
         c.start()
@@ -184,6 +300,7 @@
         return carry
 
     lax.fori_loop(0, NHEAD, forward, 0)
+    ogt[...] = pog[...].T
 
     narrow = lane_block(8)
     for j in range(SPREAD):
@@ -236,31 +353,6 @@
     recv3[me] = send3[me]
     copies3 = exchange(2, send3, recv3)
     for c in copies3:
-        c.start()
-
-    arrive(1, send2, recv2)
-    halves = []
-    for half in range(2):
-        out = jnp.zeros((8, 128), F32)
-        for s in range(half * 4, half * 4 + 4):
-            out = jnp.where(narrow == s % 4, shift(recv2[s], s), out)
-        halves.append(out)
-    theirs = jnp.concatenate(halves, 1)
-    for u in range(2):
-        top = sb[u, 0:1]
-        lse, _, _, delta = merge(theirs[u : u + 1], theirs[2 + u : 3 + u], sb[u, 1:2], sb[u, 2:3])
-        dq, dk, dv = backward_head(
-            qb[u], kb[u], vb[u], db[u], eb[u], ones, jnp.exp2(top - lse), delta
-        )
-        for s in range(SPREAD):
-            tile = slice(s // 4 * 128, s // 4 * 128 + 128)
-            out = jnp.zeros((DH, 128), F32)
-            for t, x in enumerate((dq, dk, dv)):
-                out = jnp.where(lane_block(DH) == t, shift(x[:, tile], t - s), out)
-            send4[s, u * DH : (u + 1) * DH] = out.astype(BF16)
-    recv4[me] = send4[me]
-    copies4 = exchange(3, send4, recv4)
-    for c in copies4:
         c.start()
 
     arrive(2, send3, recv3)
@@ -294,7 +386,103 @@
                     part = other[u * DH : (u + 1) * DH] * w_b[h : h + 1, tile]
                     x = x + jnp.where(lane_block(DH) == j % 4, part, 0.0)
                 att[h * DH : (h + 1) * DH, tile] = x.astype(BF16)
-    dw_ref[...] = mm(att[...], pog[...])
+    def part(which, side):
+        rows = [
+            att[y * 2 * half_rows + which * half_rows : y * 2 * half_rows + (which + 1) * half_rows]
+            for y in range(NY)
+        ]
+        rows = jnp.concatenate(rows, 0)
+        if which == 0:
+            return mm(rows, pog[:, pl.ds(pl.multiple_of(side * COLH, 128), COLH)])
+        return mm_nt(ogt[pl.ds(pl.multiple_of(side * COLH, 128), COLH)], rows)
+
+    sibling = [
+        pltpu.make_async_remote_copy(
+            src_ref=c_send.at[i],
+            dst_ref=c_recv.at[i],
+            send_sem=c_sem.at[0, i],
+            recv_sem=c_sem.at[1, i],
+            device_id=(dp, 2 * mx + 1 - mc),
+            device_id_type=MESH,
+        )
+        for i in range(2)
+    ]
+    for i in range(2):
+        c_send[i] = part(i, 1 - mc).astype(BF16)
+        sibling[i].start()
+    a1 = along(NY, my, lambda y: (y * NZ + mz, me), a1_send, a1_recv, a1_sem)
+    a2 = across(a2_send, a2_recv, a2_sem)
+    b1 = across(b1_send, b1_recv, b1_sem)
+    b2 = along(NY, my, lambda y: (y * NZ + mz, me), b2_send, b2_recv, b2_sem)
+    zz = along(NZ, mz, lambda z: (my * NZ + z, me), z_send, z_recv, z_sem)
+
+    def step_a():
+        for i, (send, count, step) in enumerate(((a1_send, NY, a1), (a2_send, NX, a2))):
+            own = part(i, mc)
+            sibling[i].wait_recv()
+            own = (own + c_recv[i].astype(F32)).astype(BF16)
+            for n in range(count):
+                send[n] = own[n * COLH // count : (n + 1) * COLH // count]
+            step[0]()
+
+    def step_b():
+        a1[1]()
+        x = total(a1_recv, NY).astype(BF16)
+        x = mm_nt(x, pick_rows(NX, COLS, COLH, 128)).astype(BF16)
+        for b in range(NX):
+            b1_send[b] = x[:, b * 128 : (b + 1) * 128]
+        b1[0]()
+        a2[1]()
+        x = total(a2_recv, NX).astype(BF16)
+        x = mm_nt(x, pick_rows(NY, half_rows, COLH, wide_rows)).astype(BF16)
+        for y in range(NY):
+            b2_send[y] = x[:, y * wide_rows : (y + 1) * wide_rows]
+        b2[0]()
+
+    def step_z():
+        pick = pick_rows(NZ // 2, z_rows, wide_rows, z_pad)
+        b1[1]()
+        x = total(b1_recv, NX)
+        x = jnp.concatenate([x, jnp.zeros((wide_rows - half_rows, 128), F32)], 0)
+        x = mm(pick, x.astype(BF16)).astype(BF16)
+        for z in range(NZ // 2):
+            z_send[z] = x[z * z_pad : (z + 1) * z_pad]
+        b2[1]()
+        x = total(b2_recv, NY)
+        x = jnp.concatenate([x, jnp.zeros((128 - COLS, wide_rows), F32)], 0)
+        x = mm_nt(pick, x.astype(BF16)).astype(BF16)
+        for z in range(NZ // 2):
+            z_send[NZ // 2 + z] = x[z * z_pad : (z + 1) * z_pad]
+        zz[0]()
+
+    def finish():
+        zz[1]()
+        dw_ref[...] = total(z_recv, NZ)[:z_rows, :COLS]
+
+    arrive(1, send2, recv2)
+    halves = []
+    for half in range(2):
+        out = jnp.zeros((8, 128), F32)
+        for s in range(half * 4, half * 4 + 4):
+            out = jnp.where(narrow == s % 4, shift(recv2[s], s), out)
+        halves.append(out)
+    theirs = jnp.concatenate(halves, 1)
+    for u in range(2):
+        top = sb[u, 0:1]
+        lse, _, _, delta = merge(theirs[u : u + 1], theirs[2 + u : 3 + u], sb[u, 1:2], sb[u, 2:3])
+        dq, dk, dv = backward_head(
+            qb[u], kb[u], vb[u], db[u], eb[u], ones, jnp.exp2(top - lse), delta
+        )
+        for s in range(SPREAD):
+            tile = slice(s // 4 * 128, s // 4 * 128 + 128)
+            out = jnp.zeros((DH, 128), F32)
+            for t, x in enumerate((dq, dk, dv)):
+                out = jnp.where(lane_block(DH) == t, shift(x[:, tile], t - s), out)
+            send4[s, u * DH : (u + 1) * DH] = out.astype(BF16)
+    recv4[me] = send4[me]
+    copies4 = exchange(3, send4, recv4)
+    for c in copies4:
+        c.start()
 
     def backward(h, carry):
         dq, dk, dv = backward_head(
@@ -305,7 +493,11 @@
         dvt[h] = dv
         return carry
 
-    lax.fori_loop(0, NHEAD, backward, 0)
+    step_a()
+    lax.fori_loop(0, NHEAD // 2, backward, 0)
+    step_b()
+    lax.fori_loop(NHEAD // 2, NHEAD, backward, 0)
+    step_z()
 
     arrive(3, send4, recv4)
     for j in range(SPREAD):
@@ -320,24 +512,34 @@
     for src, dst in ((dqt, dq_ref), (dkt, dk_ref), (dvt, dv_ref)):
         dst[...] = mm_nt(back, src[...].reshape(D, SEG).astype(BF16)).astype(BF16)
 
-    for c in copies1 + copies2 + copies3 + copies4:
+    finish()
+    for c in copies1 + copies2 + copies3 + copies4 + sibling:
         c.wait_send()
+    for step in (a1, a2, b1, b2, zz):
+        step[2]()
 
 
 def on_device(queries, keys, values, out_grad, out_weight, slide_lengths):
     vmem = pl.BlockSpec(memory_space=pltpu.VMEM)
     heads = lambda n, dtype: pltpu.VMEM((n, DH, SEG), dtype)
-    dq, dk, dv, partial = pl.pallas_call(
+    half_rows = D // NY // 2
+    wide_rows = up(half_rows, 128)
+    z_rows = D // (NY * NZ)
+    z_pad = up(z_rows, 16)
+    return pl.pallas_call(
         kernel,
         out_shape=(
             jax.ShapeDtypeStruct((SEG, D), BF16),
             jax.ShapeDtypeStruct((SEG, D), BF16),
             jax.ShapeDtypeStruct((SEG, D), BF16),
-            jax.ShapeDtypeStruct((D, D), F32),
+            jax.ShapeDtypeStruct((z_rows, COLS), F32),
         ),
-        in_specs=[vmem] * 5 + [pl.BlockSpec(memory_space=pltpu.SMEM)],
+        in_specs=[pl.BlockSpec(memory_space=pl.ANY)] * 5 + [pl.BlockSpec(memory_space=pltpu.SMEM)],
         out_specs=(vmem,) * 4,
         scratch_shapes=[
+            pltpu.VMEM((SEG, D), BF16), pltpu.VMEM((SEG, D), BF16), pltpu.VMEM((SEG, D), BF16),
+            pltpu.VMEM((SEG, D), BF16), pltpu.VMEM((D, D), BF16),
+            pltpu.SemaphoreType.DMA((5,)),
             heads(NHEAD, BF16), heads(NHEAD, BF16), heads(NHEAD, BF16), heads(NHEAD, BF16),
             pltpu.VMEM((SEG, D), BF16),
             pltpu.VMEM((NHEAD, SEG, SEG), BF16),
@@ -355,14 +557,22 @@
             pltpu.VMEM((SPREAD, PAIR, 128), BF16), pltpu.VMEM((SPREAD, PAIR, 128), BF16),
             pltpu.SemaphoreType.DMA((4, SPREAD)),
             pltpu.SemaphoreType.DMA((4, SPREAD)),
+            pltpu.VMEM((D, SEG), BF16),
+            pltpu.VMEM((2, COLH, COLH), BF16), pltpu.VMEM((2, COLH, COLH), BF16),
+            pltpu.VMEM((NY, half_rows, COLH), BF16), pltpu.VMEM((NY, half_rows, COLH), BF16),
+            pltpu.VMEM((NX, COLS, COLH), BF16), pltpu.VMEM((NX, COLS, COLH), BF16),
+            pltpu.VMEM((NX, half_rows, 128), BF16), pltpu.VMEM((NX, half_rows, 128), BF16),
+            pltpu.VMEM((NY, COLS, wide_rows), BF16), pltpu.VMEM((NY, COLS, wide_rows), BF16),
+            pltpu.VMEM((NZ, z_pad, 128), BF16), pltpu.VMEM((NZ, z_pad, 128), BF16),
+            pltpu.SemaphoreType.DMA((2, 2)),
+            pltpu.SemaphoreType.DMA((2, NY)), pltpu.SemaphoreType.DMA((2, NX)),
+            pltpu.SemaphoreType.DMA((2, NX)), pltpu.SemaphoreType.DMA((2, NY)),
+            pltpu.SemaphoreType.DMA((2, NZ)),
         ],
         compiler_params=pltpu.CompilerParams(
             collective_id=0, has_side_effects=True, vmem_limit_bytes=48 * 1024 * 1024
         ),
     )(queries, keys, values, out_grad, out_weight, slide_lengths)
-    rows_mine = lax.psum_scatter(partial, "dp", scatter_dimension=0, tiled=True)
-    weight_grad = lax.psum_scatter(rows_mine, "seq", scatter_dimension=1, tiled=True)
-    return dq, dk, dv, weight_grad
 
 
 def solution(mesh):

time: 331 us -> 60.8 us (0.18)
  blocking collectives: 136 us -> 0 us
  waiting for transfers between devices: 70.8 us -> 0 us
  starting transfers between devices: 63.4 us -> 0 us
  Pallas kernels: 30.8 us -> 51.1 us
  between operations: 15 us -> 0.66 us
  local copies, waits for them, and re-layouts: 13.9 us -> 8.74 us
    unnamed x1 -> x0, blocking collectives: 136 us -> none
    unnamed x18 -> x0, waiting for transfers between devices: 70.8 us -> none
    unnamed x17 -> x0, starting transfers between devices: 63.4 us -> none
    pallas_call x1, Pallas kernels: 30.8 us -> 51.1 us  [on_device(): pl.pallas_call(kernel, out_shape=(jax.ShapeDtypeStruct((SEG, D), BF16), j...]
    unnamed x21 -> x16, local copies, waits for them, and re-layouts: 13.9 us -> 8.74 us
  transfers between devices with their start and end apart: 17 -> 0, of which waited for: 1 -> 0; matrix products, arithmetic and copies ran while one was open for 0% -> 0% of each run, Pallas kernels for 0% -> 0%
where the time goes in v2:
time: 60.8 us; the launch traced here: 60.5 us
  Pallas kernels  51.1 us (84%)
  local copies, waits for them, and re-layouts  8.74 us (14%)
  between operations  0.66 us (1%)
    pallas_call x1, Pallas kernels, on_device(): pl.pallas_call(kernel, out_shape=(jax.ShapeDtypeStruct((SEG, D), BF16), j...  51.1 us
    unnamed x16, local copies, waits for them, and re-layouts  8.74 us

profile of v2, /device:TPU:1, one launch (start us, length us, event | category | flops | bytes accessed | tf_op | source)
XLA Modules:
  0.0 60.5 jit_solution(6852747886344647462)
XLA Ops:
  0.6 0.0 copy-start
  0.6 1.3 %copy-done = bf16[768,768]{1,0:T(8,128)(2,1)S(1)} copy-done((bf16[768,768]{1,0:T(8,128)(2,1)S(1)}, bf16[768,768]{1,0:T(8,128)(2,1)}, u32[]{:S(2)}) %copy-start) | copy-done | bytes 1179672
  1.9 0.0 copy-start.1
  1.9 1.0 %copy-done.1 = bf16[256,768]{1,0:T(8,128)(2,1)S(1)} copy-done((bf16[256,768]{1,0:T(8,128)(2,1)S(1)}, bf16[256,768]{1,0:T(8,128)(2,1)}, u32[]{:S(2)}) %copy-start.1) | copy-done | bytes 393240
  2.9 0.0 copy-start.2
  2.9 1.0 %copy-done.2 = bf16[256,768]{1,0:T(8,128)(2,1)S(1)} copy-done((bf16[256,768]{1,0:T(8,128)(2,1)S(1)}, bf16[256,768]{1,0:T(8,128)(2,1)}, u32[]{:S(2)}) %copy-start.2) | copy-done | bytes 393240
  3.9 0.0 copy-start.3
  3.9 1.0 %copy-done.3 = bf16[256,768]{1,0:T(8,128)(2,1)S(1)} copy-done((bf16[256,768]{1,0:T(8,128)(2,1)S(1)}, bf16[256,768]{1,0:T(8,128)(2,1)}, u32[]{:S(2)}) %copy-start.3) | copy-done | bytes 393240
  4.9 0.0 copy-start.4
  4.9 1.0 %copy-done.4 = bf16[256,768]{1,0:T(8,128)(2,1)S(1)} copy-done((bf16[256,768]{1,0:T(8,128)(2,1)S(1)}, bf16[256,768]{1,0:T(8,128)(2,1)}, u32[]{:S(2)}) %copy-start.4) | copy-done | bytes 393240
  5.9 0.0 copy-start.5
  5.9 0.7 %copy-done.5 = s32[1,4]{1,0:T(1,128)S(1)} copy-done((s32[1,4]{1,0:T(1,128)S(1)}, s32[1,4]{1,0:T(1,128)}, u32[]{:S(2)}) %copy-start.5) | copy-done | bytes 40
  6.5 51.1 %shard_map.93 = (bf16[256,768]{1,0:T(8,128)(2,1)S(1)}, bf16[256,768]{1,0:T(8,128)(2,1)S(1)}, bf16[256,768]{1,0:T(8,128)(2,1)S(1)}, f32[12,96]{1,0:T(8,128)S(1)}) custom-call(bf16[256,768]{1,0:T(8,128)(2,1)S(1)} %copy-done.1, bf16[256,768]{1,0:T(8,128)(2,1)S(1)} %copy-done.2, bf16[256,768]{1,0:T(8,128)(2,1)S(1)} %copy-done.3, bf16[256,768]{1,0:T(8,128)(2,1)S(1)} %copy-done.4, ...), custom_call_target="tpu_custom_call" | custom-call | tf_op jit(solution)/shard_map/pallas_call | solution.py:529
  57.7 0.7 %copy.14 = bf16[256,768]{1,0:T(8,128)(2,1)} copy(bf16[256,768]{1,0:T(8,128)(2,1)S(1)} %get-tuple-element.8) | data formatting | bytes 786432
  58.4 0.7 %copy.15 = bf16[256,768]{1,0:T(8,128)(2,1)} copy(bf16[256,768]{1,0:T(8,128)(2,1)S(1)} %get-tuple-element.9) | data formatting | bytes 786432
  59.2 0.7 %copy.16 = bf16[256,768]{1,0:T(8,128)(2,1)} copy(bf16[256,768]{1,0:T(8,128)(2,1)S(1)} %get-tuple-element.10) | data formatting | bytes 786432
  59.9 0.6 copy.17
Async XLA Ops:
  0.6 1.3 %copy-start = (bf16[768,768]{1,0:T(8,128)(2,1)S(1)}, bf16[768,768]{1,0:T(8,128)(2,1)}, u32[]{:S(2)}) copy-start(bf16[768,768]{1,0:T(8,128)(2,1)} %w_in.1) | copy-start | bytes 3538948
  1.9 1.0 %copy-start.1 = (bf16[256,768]{1,0:T(8,128)(2,1)S(1)}, bf16[256,768]{1,0:T(8,128)(2,1)}, u32[]{:S(2)}) copy-start(bf16[256,768]{1,0:T(8,128)(2,1)} %q_in.1) | copy-start | bytes 1179652
  2.9 1.0 %copy-start.2 = (bf16[256,768]{1,0:T(8,128)(2,1)S(1)}, bf16[256,768]{1,0:T(8,128)(2,1)}, u32[]{:S(2)}) copy-start(bf16[256,768]{1,0:T(8,128)(2,1)} %k_in.1) | copy-start | bytes 1179652
  3.9 1.0 %copy-start.3 = (bf16[256,768]{1,0:T(8,128)(2,1)S(1)}, bf16[256,768]{1,0:T(8,128)(2,1)}, u32[]{:S(2)}) copy-start(bf16[256,768]{1,0:T(8,128)(2,1)} %v_in.1) | copy-start | bytes 1179652
  4.9 1.0 %copy-start.4 = (bf16[256,768]{1,0:T(8,128)(2,1)S(1)}, bf16[256,768]{1,0:T(8,128)(2,1)}, u32[]{:S(2)}) copy-start(bf16[256,768]{1,0:T(8,128)(2,1)} %g_in.1) | copy-start | bytes 1179652
  5.9 0.7 %copy-start.5 = (s32[1,4]{1,0:T(1,128)S(1)}, s32[1,4]{1,0:T(1,128)}, u32[]{:S(2)}) copy-start(s32[1,4]{1,0:T(1,128)} %len_ref.1) | copy-start | bytes 52

commit v3 on v2

--- a/solution.py
+++ b/solution.py
@@ -15,14 +15,20 @@
 SPREAD = 8
 CLS = SEG // SPREAD
 PAIR = 2 * DH
+DENSE = PAIR // 4
+PACK1 = 32
+PACK3 = 80
 SLIDES = 4
 NX = 4
+UF = 8
+UB = 8
 NY = 4
 NZ = 16
 COLS = D // SPREAD
 COLH = D // 2
 PAD = 16
 BIG = 2.0**20
+VMEM_LIMIT = 60 * 1024 * 1024
 LOG2E = 1.4426950408889634
 SCALE = DH**-0.5
 F32 = jnp.float32
@@ -56,17 +62,21 @@
     return hit.astype(BF16), off.astype(BF16)
 
 
-def forward_head(qt, kt, vt, dot, k_mask, q_mask, ones):
-    s = mm_tn(jnp.concatenate([kt, k_mask], 0), jnp.concatenate([qt, q_mask], 0))
-    top = jnp.max(s, 0, keepdims=True)
-    e = jnp.exp2((s - top) * (SCALE * LOG2E)).astype(BF16)
+def scores(qt, kt, k_mask, q_mask):
+    return mm_tn(jnp.concatenate([kt, k_mask], 0), jnp.concatenate([qt, q_mask], 0))
+
+
+def weigh(s, top, vt, ones):
+    top = top * (SCALE * LOG2E)
+    e = jnp.exp2(s * (SCALE * LOG2E) - top).astype(BF16)
     ov = mm(jnp.concatenate([vt, ones], 0), e)
     total = ov[DH : DH + 1]
-    o = ov[:DH] * (1.0 / total)
-    top = top * (SCALE * LOG2E)
-    lse = top + jnp.log(total) * LOG2E
-    delta = jnp.sum(dot.astype(F32) * o, 0, keepdims=True)
-    return e, o, top, lse, delta
+    return e, ov[:DH] * (1.0 / total), top, top + jnp.log(total) * LOG2E
+
+
+def forward_head(qt, kt, vt, k_mask, q_mask, ones):
+    s = scores(qt, kt, k_mask, q_mask)
+    return weigh(s, jnp.max(s, 0, keepdims=True), vt, ones)
 
 
 def backward_head(qt, kt, vt, dot, e, ones, ratio, delta):
@@ -110,14 +120,31 @@
     return x if blocks == 0 else pltpu.roll(x, blocks * CLS, 1)
 
 
+def pack(parts, j, rows):
+    out = []
+    block = lane_block(DENSE)
+    for x in parts:
+        dense = jnp.zeros((DENSE, 128), F32)
+        for b in range(4):
+            dense = jnp.where(block == b, shift(x[b * DENSE : (b + 1) * DENSE], b - j), dense)
+        out.append(dense)
+    out.append(jnp.zeros((rows - len(parts) * DENSE, 128), F32))
+    return jnp.concatenate(out, 0)
+
+
+def unpack(x, t, j):
+    x = x[t * DENSE : (t + 1) * DENSE]
+    return jnp.concatenate([shift(x, j - b) for b in range(4)], 0)
+
+
 def kernel(
     q_in, k_in, v_in, g_in, w_in, len_ref,
-    dq_ref, dk_ref, dv_ref, dw_ref,
-    q_ref, k_ref, v_ref, g_ref, w_ref, isem,
-    qt, kt, vt, dot, pog, e_all, ot, sta, att, dqt, dkt, dvt,
+    grads_ref, dw_ref,
+    q_ref, k_ref, v_ref, g_ref, w_ref, isem, grads, osem,
+    qt, kt, vt, dot, s_all, e_all, ot, sta, att, dqt, dkt, dvt,
     qb, kb, vb, db, eb, ob, sb,
-    send1, recv1, send2, recv2, send3, recv3, send4, recv4,
-    ssem, rsem,
+    gb, send0, recv0, send1, recv1, send2, recv2, send3, recv3, send4, recv4, send5, recv5,
+    ssem, rsem, pick_x, pick_y, pick_z,
     ogt, c_send, c_recv, a1_send, a1_recv, a2_send, a2_recv, b1_send, b1_recv, b2_send, b2_recv,
     z_send, z_recv, c_sem, a1_sem, a2_sem, b1_sem, b2_sem, z_sem,
 ):
@@ -168,6 +195,7 @@
                     device_id_type=MESH,
                 )
             )
+            copies[-1].start()
         return copies
 
     def arrive(kind, send, recv):
@@ -256,51 +284,64 @@
             out = out + recv[i].astype(F32)
         return out
 
-    to = iota((SEG, SEG), 0)
-    at = iota((SEG, SEG), 1)
+    to = iota((SEG, SEG), 1)
+    at = iota((SEG, SEG), 0)
     perm = jnp.where(at == to % CLS * SPREAD + to // CLS, 1.0, 0.0).astype(BF16)
     for i, (src, dst) in enumerate(((q_ref, qt), (k_ref, kt), (v_ref, vt))):
         loads[i].wait()
-        moved = mm(perm, src[...]).T.astype(BF16)
-        dst[...] = moved.reshape(NHEAD, DH, SEG)
+        dst[...] = mm_tn(src[...], perm).astype(BF16).reshape(NHEAD, DH, SEG)
+    def class_rows(src, j):
+        tile = pl.ds(j // 4 * 128, 128)
+        both = jnp.concatenate([src[j, :, tile], src[j + SPREAD, :, tile]], 0)
+        return both.astype(F32)
+
+    for j in range(SPREAD):
+        send0[j] = pack([class_rows(x, j) for x in (qt, kt, vt)], j, PACK3).astype(BF16)
+    recv0[me] = send0[me]
+    pl.semaphore_wait(barrier, SPREAD - 1 + NY - 1 + NZ - 1)
+    copies = exchange(0, send0, recv0)
+
     loads[3].wait()
+    ogt[...] = mm_tn(g_ref[...], perm).astype(BF16)
     loads[4].wait()
-    pog[...] = mm(perm, g_ref[...]).astype(BF16)
-    dot[...] = mm_nt(w_ref[...], pog[...]).astype(BF16).reshape(NHEAD, DH, SEG)
-
-    block = lane_block(PAIR)
+    dot[...] = mm(w_ref[...], ogt[...]).astype(BF16).reshape(NHEAD, DH, SEG)
     for j in range(SPREAD):
-        tile = pl.ds(j // 4 * 128, 128)
-        out = jnp.zeros((PAIR, 128), F32)
-        for t, src in enumerate((qt, kt, vt, dot)):
-            both = jnp.concatenate([src[j, :, tile], src[j + SPREAD, :, tile]], 0)
-            out = jnp.where(block == t, shift(both.astype(F32), t - j), out)
-        send1[j] = out.astype(BF16)
+        send1[j] = pack([class_rows(dot, j)], j, PACK1).astype(BF16)
     recv1[me] = send1[me]
-
-    pl.semaphore_wait(barrier, SPREAD - 1 + NY - 1 + NZ - 1)
-    copies1 = exchange(0, send1, recv1)
-    for c in copies1:
-        c.start()
+    copies += exchange(1, send1, recv1)
+    pick_x[...] = pick_rows(NX, COLS, COLH, 128)
+    pick_y[...] = pick_rows(NY, half_rows, COLH, wide_rows)
+    pick_z[...] = pick_rows(NZ // 2, z_rows, wide_rows, z_pad)
 
     lane = iota((1, SEG), 1)
     k_mask, q_mask = mask_rows(me * SEG + lane % CLS * SPREAD + lane // CLS, ends)
     row = iota((PAD, SEG), 0)
     ones = jnp.where(row < 2, 1.0, 0.0).astype(BF16)
 
-    def forward(h, carry):
-        e, o, top, lse, delta = forward_head(
-            qt[h], kt[h], vt[h], dot[h], k_mask, q_mask, ones
-        )
+    def forward_s(h):
+        s = scores(qt[h], kt[h], k_mask, q_mask)
+        s_all[h] = s
+        sta[h, 0:1] = jnp.max(s, 0, keepdims=True)
+
+    def forward_o(h):
+        e, o, top, lse = weigh(s_all[h], sta[h, 0:1], vt[h], ones)
         e_all[h] = e
         ot[h] = o
+        att[pl.ds(pl.multiple_of(h * DH, 16), DH)] = o.astype(BF16)
         sta[h, 0:1] = top
         sta[h, 1:2] = lse
-        sta[h, 2:3] = delta
-        return carry
-
-    lax.fori_loop(0, NHEAD, forward, 0)
-    ogt[...] = pog[...].T
+        sta[h, 2:3] = jnp.sum(dot[h].astype(F32) * o, 0, keepdims=True)
+
+    def loop(body, first, last, unroll):
+        def step(i, carry):
+            for u in range(unroll):
+                body(i * unroll + u)
+            return carry
+
+        lax.fori_loop(first // unroll, last // unroll, step, 0)
+
+    loop(forward_s, 0, NHEAD, UF)
+    loop(forward_o, 0, NHEAD, UF)
 
     narrow = lane_block(8)
     for j in range(SPREAD):
@@ -311,51 +352,52 @@
              jnp.zeros((4, 128), F32)], 0)
         send2[j] = shift(rows, -j)
     recv2[me] = send2[me]
-    copies2 = exchange(1, send2, recv2)
-    for c in copies2:
-        c.start()
-
-    arrive(0, send1, recv1)
-    for half in range(2):
-        tile = pl.ds(half * 128, 128)
-        outs = [jnp.zeros((PAIR, 128), F32)] * 4
-        for s in range(half * 4, half * 4 + 4):
-            got = recv1[s].astype(F32)
-            for t in range(4):
-                outs[t] = jnp.where(block == s % 4, shift(got, s - t), outs[t])
-        for dst, out in zip((qb, kb, vb, db), outs):
-            out = out.astype(BF16)
-            for u in range(2):
-                dst[u, :, tile] = out[u * DH : (u + 1) * DH]
+    copies += exchange(2, send2, recv2)
+
+    block = lane_block(PAIR)
+
+    def gather(recv, dsts):
+        for half in range(2):
+            tile = pl.ds(half * 128, 128)
+            outs = [jnp.zeros((PAIR, 128), F32)] * len(dsts)
+            for s in range(half * 4, half * 4 + 4):
+                got = recv[s].astype(F32)
+                for t in range(len(dsts)):
+                    outs[t] = jnp.where(block == s % 4, unpack(got, t, s), outs[t])
+            for dst, out in zip(dsts, outs):
+                out = out.astype(BF16)
+                for u in range(2):
+                    dst[u, :, tile] = out[u * DH : (u + 1) * DH]
+
+    arrive(0, send0, recv0)
+    gather(recv0, (qb, kb, vb))
     kb_mask, qb_mask = mask_rows(lane * SPREAD + me, ends)
     for u in range(2):
-        e, o, top, lse, delta = forward_head(
-            qb[u], kb[u], vb[u], db[u], kb_mask, qb_mask, ones
-        )
+        e, o, top, lse = forward_head(qb[u], kb[u], vb[u], kb_mask, qb_mask, ones)
         eb[u] = e
         ob[u] = o
         sb[u, 0:1] = top
         sb[u, 1:2] = lse
-        sb[u, 2:3] = delta
-
-    wide = lane_block(CLS)
+    for s in range(SPREAD):
+        tile = pl.ds(s // 4 * 128, 128)
+        both = jnp.concatenate([ob[0, :, tile], ob[1, :, tile]], 0)
+        send3[s] = pack([both], s, PACK1).astype(BF16)
+    recv3[me] = send3[me]
+    copies += exchange(3, send3, recv3)
+    arrive(1, send1, recv1)
+    gather(recv1, (db,))
+    for u in range(2):
+        sb[u, 2:3] = jnp.sum(db[u].astype(F32) * ob[u], 0, keepdims=True)
     for s in range(SPREAD):
         tile = pl.ds(s // 4 * 128, 128)
         rows = jnp.concatenate(
             [sb[0, 1:2, tile], sb[1, 1:2, tile], sb[0, 2:3, tile], sb[1, 2:3, tile],
              jnp.zeros((4, 128), F32)], 0)
-        both = jnp.concatenate([ob[0, :, tile], ob[1, :, tile]], 0)
-        out = jnp.zeros((CLS, 128), F32)
-        for g in range(3):
-            out = jnp.where(wide == g, shift(both[g * CLS : (g + 1) * CLS], g - s), out)
-        stat = jnp.concatenate([shift(rows, 3 - s), jnp.zeros((CLS - 8, 128), F32)], 0)
-        send3[s] = jnp.where(wide == 3, stat, out)
-    recv3[me] = send3[me]
-    copies3 = exchange(2, send3, recv3)
-    for c in copies3:
-        c.start()
-
-    arrive(2, send3, recv3)
+        send4[s] = shift(rows, -s)
+    recv4[me] = send4[me]
+    copies += exchange(4, send4, recv4)
+
+    arrive(4, send4, recv4)
     tall = iota((NHEAD, 128), 0)
     spot = lane_block(NHEAD)
     lse_b, delta_b = [], []
@@ -363,7 +405,7 @@
         lb = jnp.full((NHEAD, 128), -1e30, F32)
         dbl = jnp.zeros((NHEAD, 128), F32)
         for j in range(half * 4, half * 4 + 4):
-            x = shift(recv3[j, 0:8], j - 3)
+            x = shift(recv4[j], j)
             for u in range(2):
                 here = (tall == j + SPREAD * u) & (spot == j % 4)
                 lb = jnp.where(here, x[u : u + 1], lb)
@@ -374,18 +416,17 @@
     lse, w_a, w_b, delta = merge(sta[:, 1, :], sta[:, 2, :], lse_b, delta_b)
     sta[:, 2, :] = delta
     sta[:, 3, :] = jnp.exp2(sta[:, 0, :] - lse)
+    arrive(3, send3, recv3)
     for j in range(SPREAD):
-        got = recv3[j]
-        other = jnp.concatenate([shift(got, j - g) for g in range(3)], 0)
+        other = unpack(recv3[j].astype(F32), 0, j)
+        tile = slice(j // 4 * 128, j // 4 * 128 + 128)
         for u in range(2):
             h = j + SPREAD * u
-            for half in range(2):
-                tile = slice(half * 128, half * 128 + 128)
-                x = ot[h, :, tile] * w_a[h : h + 1, tile]
-                if half == j // 4:
-                    part = other[u * DH : (u + 1) * DH] * w_b[h : h + 1, tile]
-                    x = x + jnp.where(lane_block(DH) == j % 4, part, 0.0)
-                att[h * DH : (h + 1) * DH, tile] = x.astype(BF16)
+            mine = ot[h, :, tile]
+            both = mine * w_a[h : h + 1, tile] + other[u * DH : (u + 1) * DH] * w_b[h : h + 1, tile]
+            x = jnp.where(lane_block(DH) == j % 4, both, mine)
+            att[h * DH : (h + 1) * DH, tile] = x.astype(BF16)
+
     def part(which, side):
         rows = [
             att[y * 2 * half_rows + which * half_rows : y * 2 * half_rows + (which + 1) * half_rows]
@@ -393,7 +434,7 @@
         ]
         rows = jnp.concatenate(rows, 0)
         if which == 0:
-            return mm(rows, pog[:, pl.ds(pl.multiple_of(side * COLH, 128), COLH)])
+            return mm_nt(rows, ogt[pl.ds(pl.multiple_of(side * COLH, 128), COLH)])
         return mm_nt(ogt[pl.ds(pl.multiple_of(side * COLH, 128), COLH)], rows)
 
     sibling = [
@@ -428,38 +469,37 @@
     def step_b():
         a1[1]()
         x = total(a1_recv, NY).astype(BF16)
-        x = mm_nt(x, pick_rows(NX, COLS, COLH, 128)).astype(BF16)
+        x = mm_nt(x, pick_x[...]).astype(BF16)
         for b in range(NX):
             b1_send[b] = x[:, b * 128 : (b + 1) * 128]
         b1[0]()
         a2[1]()
         x = total(a2_recv, NX).astype(BF16)
-        x = mm_nt(x, pick_rows(NY, half_rows, COLH, wide_rows)).astype(BF16)
+        x = mm_nt(x, pick_y[...]).astype(BF16)
         for y in range(NY):
             b2_send[y] = x[:, y * wide_rows : (y + 1) * wide_rows]
         b2[0]()
 
     def step_z():
-        pick = pick_rows(NZ // 2, z_rows, wide_rows, z_pad)
         b1[1]()
         x = total(b1_recv, NX)
         x = jnp.concatenate([x, jnp.zeros((wide_rows - half_rows, 128), F32)], 0)
-        x = mm(pick, x.astype(BF16)).astype(BF16)
+        x = mm(pick_z[...], x.astype(BF16)).astype(BF16)
         for z in range(NZ // 2):
             z_send[z] = x[z * z_pad : (z + 1) * z_pad]
         b2[1]()
         x = total(b2_recv, NY)
         x = jnp.concatenate([x, jnp.zeros((128 - COLS, wide_rows), F32)], 0)
-        x = mm_nt(pick, x.astype(BF16)).astype(BF16)
+        x = mm_nt(pick_z[...], x.astype(BF16)).astype(BF16)
         for z in range(NZ // 2):
             z_send[NZ // 2 + z] = x[z * z_pad : (z + 1) * z_pad]
         zz[0]()
 
     def finish():
         zz[1]()
-        dw_ref[...] = total(z_recv, NZ)[:z_rows, :COLS]
-
-    arrive(1, send2, recv2)
+        dw_ref[...] = total(z_recv, NZ)
+
+    arrive(2, send2, recv2)
     halves = []
     for half in range(2):
         out = jnp.zeros((8, 128), F32)
@@ -470,53 +510,67 @@
     for u in range(2):
         top = sb[u, 0:1]
         lse, _, _, delta = merge(theirs[u : u + 1], theirs[2 + u : 3 + u], sb[u, 1:2], sb[u, 2:3])
-        dq, dk, dv = backward_head(
+        grads_b = backward_head(
             qb[u], kb[u], vb[u], db[u], eb[u], ones, jnp.exp2(top - lse), delta
         )
-        for s in range(SPREAD):
-            tile = slice(s // 4 * 128, s // 4 * 128 + 128)
-            out = jnp.zeros((DH, 128), F32)
-            for t, x in enumerate((dq, dk, dv)):
-                out = jnp.where(lane_block(DH) == t, shift(x[:, tile], t - s), out)
-            send4[s, u * DH : (u + 1) * DH] = out.astype(BF16)
-    recv4[me] = send4[me]
-    copies4 = exchange(3, send4, recv4)
-    for c in copies4:
-        c.start()
-
-    def backward(h, carry):
+        for t in range(3):
+            gb[t, u * DH : (u + 1) * DH] = grads_b[t]
+    for s in range(SPREAD):
+        tile = pl.ds(s // 4 * 128, 128)
+        send5[s] = pack([gb[t, :, tile] for t in range(3)], s, PACK3).astype(BF16)
+    recv5[me] = send5[me]
+
+    def backward(h):
         dq, dk, dv = backward_head(
             qt[h], kt[h], vt[h], dot[h], e_all[h], ones, sta[h, 3:4], sta[h, 2:3]
         )
         dqt[h] = dq
         dkt[h] = dk
         dvt[h] = dv
-        return carry
 
     step_a()
-    lax.fori_loop(0, NHEAD // 2, backward, 0)
+    copies += exchange(5, send5, recv5)
+    loop(backward, 0, NHEAD // 2, UB)
     step_b()
-    lax.fori_loop(NHEAD // 2, NHEAD, backward, 0)
+    loop(backward, NHEAD // 2, NHEAD, UB)
     step_z()
 
-    arrive(3, send4, recv4)
+    arrive(5, send5, recv5)
     for j in range(SPREAD):
         tile = pl.ds(j // 4 * 128, 128)
-        got = recv4[j].astype(F32)
+        got = recv5[j].astype(F32)
         for t, dst in enumerate((dqt, dkt, dvt)):
-            part = jnp.where(block == j % 4, shift(got, j - t), 0.0)
+            part = jnp.where(block == j % 4, unpack(got, t, j), 0.0)
             for u in range(2):
                 h = j + SPREAD * u
                 dst[h, :, tile] = dst[h, :, tile] + part[u * DH : (u + 1) * DH]
-    back = jnp.where(to == at % CLS * SPREAD + at // CLS, 1.0, 0.0).astype(BF16)
-    for src, dst in ((dqt, dq_ref), (dkt, dk_ref), (dvt, dv_ref)):
-        dst[...] = mm_nt(back, src[...].reshape(D, SEG).astype(BF16)).astype(BF16)
+    stores = []
+    for t, src in enumerate((dqt, dkt, dvt)):
+        grads[t] = mm_nt(perm, src[...].reshape(D, SEG).astype(BF16)).astype(BF16)
+        stores.append(pltpu.make_async_copy(grads.at[t], grads_ref.at[t], osem.at[t]))
+        stores[-1].start()
 
     finish()
-    for c in copies1 + copies2 + copies3 + copies4 + sibling:
+    for c in stores:
+        c.wait()
+    for c in copies + sibling:
         c.wait_send()
     for step in (a1, a2, b1, b2, zz):
         step[2]()
+
+
+def final_kernel(grads_ref, part_ref, dq_ref, dk_ref, dv_ref, dw_ref, x, isem, osem):
+    loads = [pltpu.make_async_copy(grads_ref.at[t], x.at[t], isem.at[t]) for t in range(3)]
+    for c in loads:
+        c.start()
+    dw_ref[...] = part_ref[0 : dw_ref.shape[0], 0 : dw_ref.shape[1]]
+    stores = []
+    for t, dst in enumerate((dq_ref, dk_ref, dv_ref)):
+        loads[t].wait()
+        stores.append(pltpu.make_async_copy(x.at[t], dst, osem.at[t]))
+        stores[-1].start()
+    for c in stores:
+        c.wait()
 
 
 def on_device(queries, keys, values, out_grad, out_weight, slide_lengths):
@@ -526,22 +580,22 @@
     wide_rows = up(half_rows, 128)
     z_rows = D // (NY * NZ)
     z_pad = up(z_rows, 16)
-    return pl.pallas_call(
+    grads, partial = pl.pallas_call(
         kernel,
         out_shape=(
-            jax.ShapeDtypeStruct((SEG, D), BF16),
-            jax.ShapeDtypeStruct((SEG, D), BF16),
-            jax.ShapeDtypeStruct((SEG, D), BF16),
-            jax.ShapeDtypeStruct((z_rows, COLS), F32),
+            jax.ShapeDtypeStruct((3, SEG, D), BF16),
+            jax.ShapeDtypeStruct((z_pad, 128), F32),
         ),
         in_specs=[pl.BlockSpec(memory_space=pl.ANY)] * 5 + [pl.BlockSpec(memory_space=pltpu.SMEM)],
-        out_specs=(vmem,) * 4,
+        out_specs=(pl.BlockSpec(memory_space=pl.ANY), vmem),
         scratch_shapes=[
             pltpu.VMEM((SEG, D), BF16), pltpu.VMEM((SEG, D), BF16), pltpu.VMEM((SEG, D), BF16),
             pltpu.VMEM((SEG, D), BF16), pltpu.VMEM((D, D), BF16),
             pltpu.SemaphoreType.DMA((5,)),
+            pltpu.VMEM((3, SEG, D), BF16),
+            pltpu.SemaphoreType.DMA((3,)),
             heads(NHEAD, BF16), heads(NHEAD, BF16), heads(NHEAD, BF16), heads(NHEAD, BF16),
-            pltpu.VMEM((SEG, D), BF16),
+            pltpu.VMEM((NHEAD, SEG, SEG), F32),
             pltpu.VMEM((NHEAD, SEG, SEG), BF16),
             heads(NHEAD, F32),
             pltpu.VMEM((NHEAD, 8, SEG), F32),
@@ -551,12 +605,19 @@
             pltpu.VMEM((2, SEG, SEG), BF16),
             heads(2, F32),
             pltpu.VMEM((2, 8, SEG), F32),
-            pltpu.VMEM((SPREAD, PAIR, 128), BF16), pltpu.VMEM((SPREAD, PAIR, 128), BF16),
-            pltpu.VMEM((SPREAD, 8, 128), F32), pltpu.VMEM((SPREAD, 8, 128), F32),
-            pltpu.VMEM((SPREAD, CLS, 128), F32), pltpu.VMEM((SPREAD, CLS, 128), F32),
-            pltpu.VMEM((SPREAD, PAIR, 128), BF16), pltpu.VMEM((SPREAD, PAIR, 128), BF16),
-            pltpu.SemaphoreType.DMA((4, SPREAD)),
-            pltpu.SemaphoreType.DMA((4, SPREAD)),
+            pltpu.VMEM((3, PAIR, SEG), F32),
+            *[
+                pltpu.VMEM((SPREAD, rows, 128), dtype)
+                for rows, dtype in (
+                    (PACK3, BF16), (PACK1, BF16), (8, F32), (PACK1, BF16), (8, F32), (PACK3, BF16)
+                )
+                for _ in range(2)
+            ],
+            pltpu.SemaphoreType.DMA((6, SPREAD)),
+            pltpu.SemaphoreType.DMA((6, SPREAD)),
+            pltpu.VMEM((NX * 128, COLH), BF16),
+            pltpu.VMEM((NY * wide_rows, COLH), BF16),
+            pltpu.VMEM((NZ // 2 * z_pad, wide_rows), BF16),
             pltpu.VMEM((D, SEG), BF16),
             pltpu.VMEM((2, COLH, COLH), BF16), pltpu.VMEM((2, COLH, COLH), BF16),
             pltpu.VMEM((NY, half_rows, COLH), BF16), pltpu.VMEM((NY, half_rows, COLH), BF16),
@@ -570,9 +631,22 @@
             pltpu.SemaphoreType.DMA((2, NZ)),
         ],
         compiler_params=pltpu.CompilerParams(
-            collective_id=0, has_side_effects=True, vmem_limit_bytes=48 * 1024 * 1024
+            collective_id=0, has_side_effects=True, vmem_limit_bytes=VMEM_LIMIT
         ),
     )(queries, keys, values, out_grad, out_weight, slide_lengths)
+    out = jax.ShapeDtypeStruct((SEG, D), BF16)
+    return pl.pallas_call(
+        final_kernel,
+        out_shape=(out, out, out, jax.ShapeDtypeStruct((z_rows, COLS), F32)),
+        in_specs=[pl.BlockSpec(memory_space=pl.ANY), vmem],
+        out_specs=(pl.BlockSpec(memory_space=pl.ANY),) * 3 + (vmem,),
+        scratch_shapes=[
+            pltpu.VMEM((3, SEG, D), BF16),
+            pltpu.SemaphoreType.DMA((3,)),
+            pltpu.SemaphoreType.DMA((3,)),
+        ],
+        compiler_params=pltpu.CompilerParams(vmem_limit_bytes=VMEM_LIMIT),
+    )(grads, partial)
 
 
 def solution(mesh):

time: 60.8 us -> 51.8 us (0.85)
  local copies, waits for them, and re-layouts: 8.74 us -> 0 us
    unnamed x16 -> x0, local copies, waits for them, and re-layouts: 8.74 us -> none
    pallas_call x1 -> x2, Pallas kernels: 51.1 us -> 50.9 us  [the longest x1 47.6 us: on_device(): pl.pallas_call(kernel, out_shape=(jax.ShapeDtypeStruct((3, SEG, D), BF16)...]
where the time goes in v3:
time: 51.8 us; the launch traced here: 51.6 us
  Pallas kernels  50.9 us (98%)
  between operations  0.64 us (1%)
    pallas_call x1, Pallas kernels, on_device(): pl.pallas_call(kernel, out_shape=(jax.ShapeDtypeStruct((3, SEG, D), BF16)...  47.6 us
    pallas_call x1, Pallas kernels, on_device(): pl.pallas_call(final_kernel, out_shape=(out, out, out, jax.ShapeDtypeStru...  3.35 us

profile of v3, /device:TPU:1, one launch (start us, length us, event | category | flops | bytes accessed | tf_op | source)
XLA Modules:
  0.0 51.6 jit_solution(12110530697425921969)
XLA Ops:
  0.6 47.6 %shard_map.93 = (bf16[3,256,768]{2,1,0:T(8,128)(2,1)}, f32[16,128]{1,0:T(8,128)}) custom-call(bf16[256,768]{1,0:T(8,128)(2,1)} %q_in.1, bf16[256,768]{1,0:T(8,128)(2,1)} %k_in.1, bf16[256,768]{1,0:T(8,128)(2,1)} %v_in.1, bf16[256,768]{1,0:T(8,128)(2,1)} %g_in.1, bf16[768,768]{1,0:T(8,128)(2,1)} %w_in.1, s32[1,4]{1,0:T(1,128)} %len_ref.1), custom_call_target="tpu_custom_call" | custom-call | tf_op jit(solution)/shard_map/pallas_call | solution.py:583
  48.2 3.3 %shard_map.94 = (bf16[256,768]{1,0:T(8,128)(2,1)}, bf16[256,768]{1,0:T(8,128)(2,1)}, bf16[256,768]{1,0:T(8,128)(2,1)}, f32[12,96]{1,0:T(8,128)}) custom-call(bf16[3,256,768]{2,1,0:T(8,128)(2,1)} %get-tuple-element.6.grads_ref, f32[16,128]{1,0:T(8,128)} %get-tuple-element.7.part_ref), custom_call_target="tpu_custom_call" | custom-call | tf_op jit(solution)/shard_map/pallas_call | solution.py:638

commit v4 on v3

--- a/solution.py
+++ b/solution.py
@@ -26,6 +26,9 @@
 NZ = 16
 COLS = D // SPREAD
 COLH = D // 2
+MAIN = 128
+REM = D // NY - MAIN
+DROWS = COLS + COLS // 2
 PAD = 16
 BIG = 2.0**20
 VMEM_LIMIT = 60 * 1024 * 1024
@@ -93,26 +96,30 @@
     return dq, dk, dv
 
 
-def merge(lse_a, delta_a, lse_b, delta_b):
+def blend(lse_a, lse_b):
     top = jnp.maximum(lse_a, lse_b)
     lse = top + jnp.log(jnp.exp2(lse_a - top) + jnp.exp2(lse_b - top)) * LOG2E
-    w_a, w_b = jnp.exp2(lse_a - lse), jnp.exp2(lse_b - lse)
-    return lse, w_a, w_b, w_a * delta_a + w_b * delta_b
+    return lse, jnp.exp2(lse_a - lse), jnp.exp2(lse_b - lse)
+
+
+def three_terms(x):
+    out = []
+    for _ in range(3):
+        out.append(x.astype(BF16).astype(F32))
+        x = x - out[-1]
+    return jnp.concatenate(out + [jnp.zeros((5, x.shape[1]), F32)], 0)
 
 
 def lane_block(rows):
     return iota((rows, 128), 1) // CLS
 
 
-def pick_rows(count, step, width, padded):
-    r = iota((count * padded, width), 0)
-    at = iota((count * padded, width), 1)
-    inside = (r % padded < step) & (at == r // padded * step + r % padded)
-    return jnp.where(inside, 1.0, 0.0).astype(BF16)
-
-
 def up(n, to):
     return (n + to - 1) // to * to
+
+
+def far_first(size):
+    return sorted(range(1, size), key=lambda d: -min(d, size - d))
 
 
 def shift(x, blocks):
@@ -128,7 +135,8 @@
         for b in range(4):
             dense = jnp.where(block == b, shift(x[b * DENSE : (b + 1) * DENSE], b - j), dense)
         out.append(dense)
-    out.append(jnp.zeros((rows - len(parts) * DENSE, 128), F32))
+    if rows > len(parts) * DENSE:
+        out.append(jnp.zeros((rows - len(parts) * DENSE, 128), F32))
     return jnp.concatenate(out, 0)
 
 
@@ -144,15 +152,13 @@
     qt, kt, vt, dot, s_all, e_all, ot, sta, att, dqt, dkt, dvt,
     qb, kb, vb, db, eb, ob, sb,
     gb, send0, recv0, send1, recv1, send2, recv2, send3, recv3, send4, recv4, send5, recv5,
-    ssem, rsem, pick_x, pick_y, pick_z,
-    ogt, c_send, c_recv, a1_send, a1_recv, a2_send, a2_recv, b1_send, b1_recv, b2_send, b2_recv,
-    z_send, z_recv, c_sem, a1_sem, a2_sem, b1_sem, b2_sem, z_sem,
+    ssem, rsem, pick_main, pick_rest,
+    ogt, att_x, lse_own, lse_x, og_x,
+    d_send, d_recv, z_send, z_recv, c_sem, d_sem, z_sem,
 ):
     dp = lax.axis_index("dp")
     me = lax.axis_index("seq")
     my, mz, mx, mc = dp // NZ, dp % NZ, me // 2, me % 2
-    half_rows = D // NY // 2
-    wide_rows = up(half_rows, 128)
     z_rows = D // (NY * NZ)
     z_pad = up(z_rows, 16)
 
@@ -161,33 +167,34 @@
         ((q_in, q_ref), (k_in, k_ref), (v_in, v_ref), (g_in, g_ref), (w_in, w_ref))
     ):
         loads.append(pltpu.make_async_copy(src, dst, isem.at[i]))
-        loads[-1].start()
+    for c in loads[:3]:
+        c.start()
 
     barrier = pltpu.get_barrier_semaphore()
+    for d in far_first(NZ):
+        pl.semaphore_signal(
+            barrier, inc=1, device_id=(my * NZ + lax.rem(mz + d, NZ), me), device_id_type=MESH
+        )
+    for d in range(1, NY):
+        for x in range(NX):
+            other = (lax.rem(my + d, NY) * NZ + mz, 2 * x + me // 4)
+            pl.semaphore_signal(barrier, inc=1, device_id=other, device_id_type=MESH)
     for d in range(1, SPREAD):
         pl.semaphore_signal(
             barrier, inc=1, device_id=(dp, lax.rem(me + d, SPREAD)), device_id_type=MESH
         )
-    for d in range(1, NY):
-        pl.semaphore_signal(
-            barrier, inc=1, device_id=(lax.rem(my + d, NY) * NZ + mz, me), device_id_type=MESH
-        )
-    for d in range(1, NZ):
-        pl.semaphore_signal(
-            barrier, inc=1, device_id=(my * NZ + lax.rem(mz + d, NZ), me), device_id_type=MESH
-        )
 
     ends = []
     for i in range(SLIDES):
         ends.append(len_ref[0, i] if i == 0 else ends[-1] + len_ref[0, i])
 
-    def exchange(kind, send, recv):
+    def exchange(kind, send, recv, group=1):
         copies = []
-        for d in range(1, SPREAD):
+        for d in far_first(SPREAD):
             other = lax.rem(me + d, SPREAD)
             copies.append(
                 pltpu.make_async_remote_copy(
-                    src_ref=send.at[other],
+                    src_ref=send.at[other // group],
                     dst_ref=recv.at[me],
                     send_sem=ssem.at[kind, d],
                     recv_sem=rsem.at[kind, d],
@@ -198,11 +205,11 @@
             copies[-1].start()
         return copies
 
-    def arrive(kind, send, recv):
+    def arrive(kind, send, recv, group=1):
         for d in range(1, SPREAD):
             source = lax.rem(me + SPREAD - d, SPREAD)
             pltpu.make_async_remote_copy(
-                src_ref=send.at[source],
+                src_ref=send.at[source // group],
                 dst_ref=recv.at[source],
                 send_sem=ssem.at[kind, d],
                 recv_sem=rsem.at[kind, d],
@@ -222,9 +229,9 @@
             )
 
         def start():
+            for d in far_first(size):
+                copy(d, place, lax.rem(place + d, size)).start()
             recv[place] = send[place]
-            for d in range(1, size):
-                copy(d, place, lax.rem(place + d, size)).start()
 
         def finish():
             for d in range(1, size):
@@ -237,46 +244,46 @@
 
         return start, finish, sent
 
-    def across(send, recv, sem):
-        def copy(b, slot, other):
-            return pltpu.make_async_remote_copy(
-                src_ref=send.at[b],
-                dst_ref=recv.at[slot],
-                send_sem=sem.at[0, b],
-                recv_sem=sem.at[1, slot],
-                device_id=(dp, other),
-                device_id_type=MESH,
-            )
-
-        def start():
+    def plane_each(do, own=None):
+        for d in (2, 1, 3, 0):
+            y = lax.rem(my + d, NY)
             for b in range(NX):
                 other = 4 * mc + b
-
-                @pl.when(other != me)
-                def _():
-                    copy(b, mx, other).start()
-
-                @pl.when(other == me)
-                def _():
-                    recv[mx] = send[b]
-
-        def finish():
+                copy = pltpu.make_async_remote_copy(
+                    src_ref=d_send.at[y * NX + b],
+                    dst_ref=d_recv.at[d * NX + mx],
+                    send_sem=d_sem.at[0, d * NX + b],
+                    recv_sem=d_sem.at[1, d * NX + mx],
+                    device_id=(y * NZ + mz, other),
+                    device_id_type=MESH,
+                )
+                if d:
+                    do(copy)
+                else:
+                    pl.when(other != me)(functools.partial(do, copy))
+                    if own is not None:
+                        pl.when(other == me)(functools.partial(own, b))
+
+    def plane_own(b):
+        d_recv[mx] = d_send[my * NX + b]
+
+    def plane_arrive():
+        for d in (0, 1, 3, 2):
+            y = lax.rem(my + NY - d, NY)
             for x in range(NX):
                 source = 2 * x + me // 4
-
-                @pl.when(source != me)
-                def _():
-                    copy(0, x, source).wait_recv()
-
-        def sent():
-            for b in range(NX):
-                other = 4 * mc + b
-
-                @pl.when(other != me)
-                def _():
-                    copy(b, mx, other).wait_send()
-
-        return start, finish, sent
+                copy = pltpu.make_async_remote_copy(
+                    src_ref=d_send.at[0],
+                    dst_ref=d_recv.at[d * NX + x],
+                    send_sem=d_sem.at[0, d * NX],
+                    recv_sem=d_sem.at[1, d * NX + x],
+                    device_id=(y * NZ + mz, source),
+                    device_id_type=MESH,
+                )
+                if d:
+                    copy.wait_recv()
+                else:
+                    pl.when(source != me)(copy.wait_recv)
 
     def total(recv, count):
         out = recv[0].astype(F32)
@@ -289,6 +296,9 @@
     perm = jnp.where(at == to % CLS * SPREAD + to // CLS, 1.0, 0.0).astype(BF16)
     for i, (src, dst) in enumerate(((q_ref, qt), (k_ref, kt), (v_ref, vt))):
         loads[i].wait()
+        if i == 0:
+            loads[3].start()
+            loads[4].start()
         dst[...] = mm_tn(src[...], perm).astype(BF16).reshape(NHEAD, DH, SEG)
     def class_rows(src, j):
         tile = pl.ds(j // 4 * 128, 128)
@@ -298,7 +308,7 @@
     for j in range(SPREAD):
         send0[j] = pack([class_rows(x, j) for x in (qt, kt, vt)], j, PACK3).astype(BF16)
     recv0[me] = send0[me]
-    pl.semaphore_wait(barrier, SPREAD - 1 + NY - 1 + NZ - 1)
+    pl.semaphore_wait(barrier, SPREAD - 1 + (NY - 1) * NX + NZ - 1)
     copies = exchange(0, send0, recv0)
 
     loads[3].wait()
@@ -309,9 +319,11 @@
         send1[j] = pack([class_rows(dot, j)], j, PACK1).astype(BF16)
     recv1[me] = send1[me]
     copies += exchange(1, send1, recv1)
-    pick_x[...] = pick_rows(NX, COLS, COLH, 128)
-    pick_y[...] = pick_rows(NY, half_rows, COLH, wide_rows)
-    pick_z[...] = pick_rows(NZ // 2, z_rows, wide_rows, z_pad)
+    z_at = iota((NZ * z_pad, 128), 0)
+    lane = iota((NZ * z_pad, 128), 1)
+    z_at = jnp.where(z_at % z_pad < z_rows, z_at // z_pad * z_rows + z_at % z_pad, -1)
+    pick_main[...] = jnp.where(lane == z_at, 1.0, 0.0).astype(BF16)
+    pick_rest[...] = jnp.where(lane + MAIN == z_at, 1.0, 0.0).astype(BF16)
 
     lane = iota((1, SEG), 1)
     k_mask, q_mask = mask_rows(me * SEG + lane % CLS * SPREAD + lane // CLS, ends)
@@ -342,6 +354,26 @@
 
     loop(forward_s, 0, NHEAD, UF)
     loop(forward_o, 0, NHEAD, UF)
+
+    lse_own[...] = sta[:, 1, :]
+    early = [
+        (att, att_x),
+        (lse_own, lse_x),
+        (ogt.at[pl.ds(pl.multiple_of((1 - mc) * COLH, 128), COLH)], og_x),
+    ]
+    sibling = [
+        pltpu.make_async_remote_copy(
+            src_ref=src,
+            dst_ref=dst,
+            send_sem=c_sem.at[0, i],
+            recv_sem=c_sem.at[1, i],
+            device_id=(dp, 2 * mx + 1 - mc),
+            device_id_type=MESH,
+        )
+        for i, (src, dst) in enumerate(early)
+    ]
+    for c in sibling:
+        c.start()
 
     narrow = lane_block(8)
     for j in range(SPREAD):
@@ -381,118 +413,110 @@
     for s in range(SPREAD):
         tile = pl.ds(s // 4 * 128, 128)
         both = jnp.concatenate([ob[0, :, tile], ob[1, :, tile]], 0)
-        send3[s] = pack([both], s, PACK1).astype(BF16)
-    recv3[me] = send3[me]
-    copies += exchange(3, send3, recv3)
+        lses = jnp.where(
+            lane_block(1) == 0, shift(sb[0, 1:2, tile], -s), shift(sb[1, 1:2, tile], 1 - s)
+        )
+        dense = jnp.concatenate([pack([both], s, DENSE), three_terms(lses)], 0)
+        send3[s // 2, s % 2] = dense.astype(BF16)
+    recv3[me] = send3[mx]
+    copies += exchange(3, send3, recv3, 2)
     arrive(1, send1, recv1)
     gather(recv1, (db,))
     for u in range(2):
         sb[u, 2:3] = jnp.sum(db[u].astype(F32) * ob[u], 0, keepdims=True)
     for s in range(SPREAD):
         tile = pl.ds(s // 4 * 128, 128)
-        rows = jnp.concatenate(
-            [sb[0, 1:2, tile], sb[1, 1:2, tile], sb[0, 2:3, tile], sb[1, 2:3, tile],
-             jnp.zeros((4, 128), F32)], 0)
+        rows = jnp.concatenate([sb[0, 2:3, tile], sb[1, 2:3, tile], jnp.zeros((6, 128), F32)], 0)
         send4[s] = shift(rows, -s)
     recv4[me] = send4[me]
     copies += exchange(4, send4, recv4)
 
-    arrive(4, send4, recv4)
     tall = iota((NHEAD, 128), 0)
     spot = lane_block(NHEAD)
-    lse_b, delta_b = [], []
-    for half in range(2):
-        lb = jnp.full((NHEAD, 128), -1e30, F32)
-        dbl = jnp.zeros((NHEAD, 128), F32)
-        for j in range(half * 4, half * 4 + 4):
-            x = shift(recv4[j], j)
+
+    def spread_rows(pairs, empty):
+        sides = []
+        for half in range(2):
+            out = jnp.full((NHEAD, 128), empty, F32)
+            for j in range(half * 4, half * 4 + 4):
+                for u in range(2):
+                    here = (tall == j + SPREAD * u) & (spot == j % 4)
+                    out = jnp.where(here, pairs[j][u], out)
+            sides.append(out)
+        return jnp.concatenate(sides, 1)
+
+    def combine(which, lse_a, target):
+        got = [recv3[j, which].astype(F32) for j in range(SPREAD)]
+        pairs = []
+        for j in range(SPREAD):
+            x = got[j][DENSE : DENSE + 1] + got[j][DENSE + 1 : DENSE + 2]
+            x = x + got[j][DENSE + 2 : DENSE + 3]
+            pairs.append((shift(x, j), shift(x, j - 1)))
+        lse, w_a, w_b = blend(lse_a, spread_rows(pairs, -1e30))
+        for j in range(SPREAD):
+            other = unpack(got[j], 0, j)
+            tile = slice(j // 4 * 128, j // 4 * 128 + 128)
             for u in range(2):
-                here = (tall == j + SPREAD * u) & (spot == j % 4)
-                lb = jnp.where(here, x[u : u + 1], lb)
-                dbl = jnp.where(here, x[2 + u : 3 + u], dbl)
-        lse_b.append(lb)
-        delta_b.append(dbl)
-    lse_b, delta_b = jnp.concatenate(lse_b, 1), jnp.concatenate(delta_b, 1)
-    lse, w_a, w_b, delta = merge(sta[:, 1, :], sta[:, 2, :], lse_b, delta_b)
-    sta[:, 2, :] = delta
+                h = j + SPREAD * u
+                mine = target[h * DH : (h + 1) * DH, tile].astype(F32)
+                both = mine * w_a[h : h + 1, tile]
+                both = both + other[u * DH : (u + 1) * DH] * w_b[h : h + 1, tile]
+                x = jnp.where(lane_block(DH) == j % 4, both, mine)
+                target[h * DH : (h + 1) * DH, tile] = x.astype(BF16)
+        return lse, w_a, w_b
+
+    for c in sibling:
+        c.wait()
+    arrive(3, send3, recv3, 2)
+    lse, w_a, w_b = combine(mc, lse_own[...], att)
+    combine(1 - mc, lse_x[...], att_x)
+
+    def part(first, count):
+        out = 0.0
+        for rows, cols in (
+            (att, ogt.at[pl.ds(pl.multiple_of(mc * COLH, 128), COLH)]),
+            (att_x, og_x),
+        ):
+            starts = [y * (MAIN + REM) + first for y in range(NY)]
+            x = jnp.concatenate([rows[i : i + count] for i in starts], 0)
+            out = out + mm_nt(cols[...], x)
+        return out
+
+    zz = along(NZ, mz, lambda z: (my * NZ + z, me), z_send, z_recv, z_sem)
+    main, rest = part(0, MAIN), part(MAIN, REM)
+    low = iota((COLS // 2, 128), 1) < REM
+    for y in range(NY):
+        for b in range(NX):
+            d_send[y * NX + b, :COLS] = main[
+                b * COLS : (b + 1) * COLS, y * MAIN : (y + 1) * MAIN
+            ].astype(BF16)
+            x = rest[b * COLS : (b + 1) * COLS, y // 2 * 128 : y // 2 * 128 + 128]
+            top, bottom = x[: COLS // 2], x[COLS // 2 :]
+            if y % 2:
+                top = pltpu.roll(top, REM, 1)
+            else:
+                bottom = pltpu.roll(bottom, REM, 1)
+            d_send[y * NX + b, COLS:] = jnp.where(low, top, bottom).astype(BF16)
+    plane_each(lambda copy: copy.start(), plane_own)
+
+    arrive(4, send4, recv4)
+    pairs = []
+    for j in range(SPREAD):
+        x = shift(recv4[j], j)
+        pairs.append((x[0:1], x[1:2]))
+    sta[:, 2, :] = w_a * sta[:, 2, :] + w_b * spread_rows(pairs, 0.0)
     sta[:, 3, :] = jnp.exp2(sta[:, 0, :] - lse)
-    arrive(3, send3, recv3)
-    for j in range(SPREAD):
-        other = unpack(recv3[j].astype(F32), 0, j)
-        tile = slice(j // 4 * 128, j // 4 * 128 + 128)
-        for u in range(2):
-            h = j + SPREAD * u
-            mine = ot[h, :, tile]
-            both = mine * w_a[h : h + 1, tile] + other[u * DH : (u + 1) * DH] * w_b[h : h + 1, tile]
-            x = jnp.where(lane_block(DH) == j % 4, both, mine)
-            att[h * DH : (h + 1) * DH, tile] = x.astype(BF16)
-
-    def part(which, side):
-        rows = [
-            att[y * 2 * half_rows + which * half_rows : y * 2 * half_rows + (which + 1) * half_rows]
-            for y in range(NY)
-        ]
-        rows = jnp.concatenate(rows, 0)
-        if which == 0:
-            return mm_nt(rows, ogt[pl.ds(pl.multiple_of(side * COLH, 128), COLH)])
-        return mm_nt(ogt[pl.ds(pl.multiple_of(side * COLH, 128), COLH)], rows)
-
-    sibling = [
-        pltpu.make_async_remote_copy(
-            src_ref=c_send.at[i],
-            dst_ref=c_recv.at[i],
-            send_sem=c_sem.at[0, i],
-            recv_sem=c_sem.at[1, i],
-            device_id=(dp, 2 * mx + 1 - mc),
-            device_id_type=MESH,
-        )
-        for i in range(2)
-    ]
-    for i in range(2):
-        c_send[i] = part(i, 1 - mc).astype(BF16)
-        sibling[i].start()
-    a1 = along(NY, my, lambda y: (y * NZ + mz, me), a1_send, a1_recv, a1_sem)
-    a2 = across(a2_send, a2_recv, a2_sem)
-    b1 = across(b1_send, b1_recv, b1_sem)
-    b2 = along(NY, my, lambda y: (y * NZ + mz, me), b2_send, b2_recv, b2_sem)
-    zz = along(NZ, mz, lambda z: (my * NZ + z, me), z_send, z_recv, z_sem)
-
-    def step_a():
-        for i, (send, count, step) in enumerate(((a1_send, NY, a1), (a2_send, NX, a2))):
-            own = part(i, mc)
-            sibling[i].wait_recv()
-            own = (own + c_recv[i].astype(F32)).astype(BF16)
-            for n in range(count):
-                send[n] = own[n * COLH // count : (n + 1) * COLH // count]
-            step[0]()
-
-    def step_b():
-        a1[1]()
-        x = total(a1_recv, NY).astype(BF16)
-        x = mm_nt(x, pick_x[...]).astype(BF16)
-        for b in range(NX):
-            b1_send[b] = x[:, b * 128 : (b + 1) * 128]
-        b1[0]()
-        a2[1]()
-        x = total(a2_recv, NX).astype(BF16)
-        x = mm_nt(x, pick_y[...]).astype(BF16)
-        for y in range(NY):
-            b2_send[y] = x[:, y * wide_rows : (y + 1) * wide_rows]
-        b2[0]()
 
     def step_z():
-        b1[1]()
-        x = total(b1_recv, NX)
-        x = jnp.concatenate([x, jnp.zeros((wide_rows - half_rows, 128), F32)], 0)
-        x = mm(pick_z[...], x.astype(BF16)).astype(BF16)
-        for z in range(NZ // 2):
+        plane_arrive()
+        x = total(d_recv, NY * NX)
+        rest = jnp.concatenate([x[COLS:], pltpu.roll(x[COLS:], REM, 1)], 0)
+        pad = jnp.zeros((128 - COLS, 128), F32)
+        x = jnp.concatenate([x[:COLS], pad], 0).astype(BF16)
+        rest = jnp.concatenate([rest, pad], 0).astype(BF16)
+        x = (mm_nt(pick_main[...], x) + mm_nt(pick_rest[...], rest)).astype(BF16)
+        for z in range(NZ):
             z_send[z] = x[z * z_pad : (z + 1) * z_pad]
-        b2[1]()
-        x = total(b2_recv, NY)
-        x = jnp.concatenate([x, jnp.zeros((128 - COLS, wide_rows), F32)], 0)
-        x = mm_nt(pick_z[...], x.astype(BF16)).astype(BF16)
-        for z in range(NZ // 2):
-            z_send[NZ // 2 + z] = x[z * z_pad : (z + 1) * z_pad]
         zz[0]()
 
     def finish():
@@ -509,7 +533,8 @@
     theirs = jnp.concatenate(halves, 1)
     for u in range(2):
         top = sb[u, 0:1]
-        lse, _, _, delta = merge(theirs[u : u + 1], theirs[2 + u : 3 + u], sb[u, 1:2], sb[u, 2:3])
+        lse, w_a, w_b = blend(theirs[u : u + 1], sb[u, 1:2])
+        delta = w_a * theirs[2 + u : 3 + u] + w_b * sb[u, 2:3]
         grads_b = backward_head(
             qb[u], kb[u], vb[u], db[u], eb[u], ones, jnp.exp2(top - lse), delta
         )
@@ -528,11 +553,8 @@
         dkt[h] = dk
         dvt[h] = dv
 
-    step_a()
     copies += exchange(5, send5, recv5)
-    loop(backward, 0, NHEAD // 2, UB)
-    step_b()
-    loop(backward, NHEAD // 2, NHEAD, UB)
+    loop(backward, 0, NHEAD, UB)
     step_z()
 
     arrive(5, send5, recv5)
@@ -553,10 +575,10 @@
     finish()
     for c in stores:
         c.wait()
-    for c in copies + sibling:
+    for c in copies:
         c.wait_send()
-    for step in (a1, a2, b1, b2, zz):
-        step[2]()
+    plane_each(lambda copy: copy.wait_send())
+    zz[2]()
 
 
 def final_kernel(grads_ref, part_ref, dq_ref, dk_ref, dv_ref, dw_ref, x, isem, osem):
@@ -576,8 +598,6 @@
 def on_device(queries, keys, values, out_grad, out_weight, slide_lengths):
     vmem = pl.BlockSpec(memory_space=pltpu.VMEM)
     heads = lambda n, dtype: pltpu.VMEM((n, DH, SEG), dtype)
-    half_rows = D // NY // 2
-    wide_rows = up(half_rows, 128)
     z_rows = D // (NY * NZ)
     z_pad = up(z_rows, 16)
     grads, partial = pl.pallas_call(
@@ -606,28 +626,24 @@
             heads(2, F32),
             pltpu.VMEM((2, 8, SEG), F32),
             pltpu.VMEM((3, PAIR, SEG), F32),
-            *[
-                pltpu.VMEM((SPREAD, rows, 128), dtype)
-                for rows, dtype in (
-                    (PACK3, BF16), (PACK1, BF16), (8, F32), (PACK1, BF16), (8, F32), (PACK3, BF16)
-                )
-                for _ in range(2)
-            ],
+            pltpu.VMEM((SPREAD, PACK3, 128), BF16), pltpu.VMEM((SPREAD, PACK3, 128), BF16),
+            pltpu.VMEM((SPREAD, PACK1, 128), BF16), pltpu.VMEM((SPREAD, PACK1, 128), BF16),
+            pltpu.VMEM((SPREAD, 8, 128), F32), pltpu.VMEM((SPREAD, 8, 128), F32),
+            pltpu.VMEM((SPREAD // 2, 2, PACK1, 128), BF16),
+            pltpu.VMEM((SPREAD, 2, PACK1, 128), BF16),
+            pltpu.VMEM((SPREAD, 8, 128), F32), pltpu.VMEM((SPREAD, 8, 128), F32),
+            pltpu.VMEM((SPREAD, PACK3, 128), BF16), pltpu.VMEM((SPREAD, PACK3, 128), BF16),
             pltpu.SemaphoreType.DMA((6, SPREAD)),
             pltpu.SemaphoreType.DMA((6, SPREAD)),
-            pltpu.VMEM((NX * 128, COLH), BF16),
-            pltpu.VMEM((NY * wide_rows, COLH), BF16),
-            pltpu.VMEM((NZ // 2 * z_pad, wide_rows), BF16),
+            pltpu.VMEM((NZ * z_pad, 128), BF16), pltpu.VMEM((NZ * z_pad, 128), BF16),
             pltpu.VMEM((D, SEG), BF16),
-            pltpu.VMEM((2, COLH, COLH), BF16), pltpu.VMEM((2, COLH, COLH), BF16),
-            pltpu.VMEM((NY, half_rows, COLH), BF16), pltpu.VMEM((NY, half_rows, COLH), BF16),
-            pltpu.VMEM((NX, COLS, COLH), BF16), pltpu.VMEM((NX, COLS, COLH), BF16),
-            pltpu.VMEM((NX, half_rows, 128), BF16), pltpu.VMEM((NX, half_rows, 128), BF16),
-            pltpu.VMEM((NY, COLS, wide_rows), BF16), pltpu.VMEM((NY, COLS, wide_rows), BF16),
+            pltpu.VMEM((D, SEG), BF16),
+            pltpu.VMEM((NHEAD, SEG), F32), pltpu.VMEM((NHEAD, SEG), F32),
+            pltpu.VMEM((COLH, SEG), BF16),
+            pltpu.VMEM((NY * NX, DROWS, 128), BF16), pltpu.VMEM((NY * NX, DROWS, 128), BF16),
             pltpu.VMEM((NZ, z_pad, 128), BF16), pltpu.VMEM((NZ, z_pad, 128), BF16),
-            pltpu.SemaphoreType.DMA((2, 2)),
-            pltpu.SemaphoreType.DMA((2, NY)), pltpu.SemaphoreType.DMA((2, NX)),
-            pltpu.SemaphoreType.DMA((2, NX)), pltpu.SemaphoreType.DMA((2, NY)),
+            pltpu.SemaphoreType.DMA((2, 3)),
+            pltpu.SemaphoreType.DMA((2, NY * NX)),
             pltpu.SemaphoreType.DMA((2, NZ)),
         ],
         compiler_params=pltpu.CompilerParams(

time: 51.8 us -> 49.9 us (0.963)
  Pallas kernels: 50.9 us -> 48.6 us
    pallas_call x1, Pallas kernels: 47.6 us -> 45.3 us  [on_device(): pl.pallas_call(kernel, out_shape=(jax.ShapeDtypeStruct((3, SEG, D), BF16)...]
where the time goes in v4:
time: 49.9 us; the launch traced here: 49.2 us
  Pallas kernels  48.6 us (97%)
  between operations  0.64 us (1%)
    pallas_call x1, Pallas kernels, on_device(): pl.pallas_call(kernel, out_shape=(jax.ShapeDtypeStruct((3, SEG, D), BF16)...  45.3 us
    pallas_call x1, Pallas kernels, on_device(): pl.pallas_call(final_kernel, out_shape=(out, out, out, jax.ShapeDtypeStru...  3.35 us

profile of v4, /device:TPU:1, one launch (start us, length us, event | category | flops | bytes accessed | tf_op | source)
XLA Modules:
  0.0 49.2 jit_solution(6135882867112160027)
XLA Ops:
  0.6 45.3 %shard_map.93 = (bf16[3,256,768]{2,1,0:T(8,128)(2,1)}, f32[16,128]{1,0:T(8,128)}) custom-call(bf16[256,768]{1,0:T(8,128)(2,1)} %q_in.1, bf16[256,768]{1,0:T(8,128)(2,1)} %k_in.1, bf16[256,768]{1,0:T(8,128)(2,1)} %v_in.1, bf16[256,768]{1,0:T(8,128)(2,1)} %g_in.1, bf16[768,768]{1,0:T(8,128)(2,1)} %w_in.1, s32[1,4]{1,0:T(1,128)} %len_ref.1), custom_call_target="tpu_custom_call" | custom-call | tf_op jit(solution)/shard_map/pallas_call | solution.py:603
  45.9 3.3 %shard_map.94 = (bf16[256,768]{1,0:T(8,128)(2,1)}, bf16[256,768]{1,0:T(8,128)(2,1)}, bf16[256,768]{1,0:T(8,128)(2,1)}, f32[12,96]{1,0:T(8,128)}) custom-call(bf16[3,256,768]{2,1,0:T(8,128)(2,1)} %get-tuple-element.6.grads_ref, f32[16,128]{1,0:T(8,128)} %get-tuple-element.7.part_ref), custom_call_target="tpu_custom_call" | custom-call | tf_op jit(solution)/shard_map/pallas_call | solution.py:654

commit v5 on v4

--- a/solution.py
+++ b/solution.py
@@ -146,9 +146,9 @@
 
 
 def kernel(
-    q_in, k_in, v_in, g_in, w_in, len_ref,
+    q_in, k_in, v_in, g_in, w_in, len_in,
     grads_ref, dw_ref,
-    q_ref, k_ref, v_ref, g_ref, w_ref, isem, grads, osem,
+    q_ref, k_ref, v_ref, g_ref, w_ref, len_ref, isem, grads, osem,
     qt, kt, vt, dot, s_all, e_all, ot, sta, att, dqt, dkt, dvt,
     qb, kb, vb, db, eb, ob, sb,
     gb, send0, recv0, send1, recv1, send2, recv2, send3, recv3, send4, recv4, send5, recv5,
@@ -164,7 +164,10 @@
 
     loads = []
     for i, (src, dst) in enumerate(
-        ((q_in, q_ref), (k_in, k_ref), (v_in, v_ref), (g_in, g_ref), (w_in, w_ref))
+        (
+            (q_in, q_ref), (k_in, k_ref), (v_in, v_ref), (g_in, g_ref), (w_in, w_ref),
+            (len_in, len_ref),
+        )
     ):
         loads.append(pltpu.make_async_copy(src, dst, isem.at[i]))
     for c in loads[:3]:
@@ -183,10 +186,6 @@
         pl.semaphore_signal(
             barrier, inc=1, device_id=(dp, lax.rem(me + d, SPREAD)), device_id_type=MESH
         )
-
-    ends = []
-    for i in range(SLIDES):
-        ends.append(len_ref[0, i] if i == 0 else ends[-1] + len_ref[0, i])
 
     def exchange(kind, send, recv, group=1):
         copies = []
@@ -297,8 +296,8 @@
     for i, (src, dst) in enumerate(((q_ref, qt), (k_ref, kt), (v_ref, vt))):
         loads[i].wait()
         if i == 0:
-            loads[3].start()
-            loads[4].start()
+            for c in loads[3:]:
+                c.start()
         dst[...] = mm_tn(src[...], perm).astype(BF16).reshape(NHEAD, DH, SEG)
     def class_rows(src, j):
         tile = pl.ds(j // 4 * 128, 128)
@@ -325,6 +324,10 @@
     pick_main[...] = jnp.where(lane == z_at, 1.0, 0.0).astype(BF16)
     pick_rest[...] = jnp.where(lane + MAIN == z_at, 1.0, 0.0).astype(BF16)
 
+    loads[5].wait()
+    ends = []
+    for i in range(SLIDES):
+        ends.append(len_ref[0, i] if i == 0 else ends[-1] + len_ref[0, i])
     lane = iota((1, SEG), 1)
     k_mask, q_mask = mask_rows(me * SEG + lane % CLS * SPREAD + lane // CLS, ends)
     row = iota((PAD, SEG), 0)
@@ -581,16 +584,20 @@
     zz[2]()
 
 
-def final_kernel(grads_ref, part_ref, dq_ref, dk_ref, dv_ref, dw_ref, x, isem, osem):
+def final_kernel(grads_ref, part_ref, dq_ref, dk_ref, dv_ref, dw_ref, x, part, dw, isem, osem):
     loads = [pltpu.make_async_copy(grads_ref.at[t], x.at[t], isem.at[t]) for t in range(3)]
+    loads.append(pltpu.make_async_copy(part_ref, part, isem.at[3]))
     for c in loads:
         c.start()
-    dw_ref[...] = part_ref[0 : dw_ref.shape[0], 0 : dw_ref.shape[1]]
     stores = []
     for t, dst in enumerate((dq_ref, dk_ref, dv_ref)):
         loads[t].wait()
         stores.append(pltpu.make_async_copy(x.at[t], dst, osem.at[t]))
         stores[-1].start()
+    loads[3].wait()
+    dw[...] = part[0 : dw.shape[0], 0 : dw.shape[1]]
+    stores.append(pltpu.make_async_copy(dw, dw_ref, osem.at[3]))
+    stores[-1].start()
     for c in stores:
         c.wait()
 
@@ -606,12 +613,13 @@
             jax.ShapeDtypeStruct((3, SEG, D), BF16),
             jax.ShapeDtypeStruct((z_pad, 128), F32),
         ),
-        in_specs=[pl.BlockSpec(memory_space=pl.ANY)] * 5 + [pl.BlockSpec(memory_space=pltpu.SMEM)],
+        in_specs=[pl.BlockSpec(memory_space=pl.ANY)] * 6,
         out_specs=(pl.BlockSpec(memory_space=pl.ANY), vmem),
         scratch_shapes=[
             pltpu.VMEM((SEG, D), BF16), pltpu.VMEM((SEG, D), BF16), pltpu.VMEM((SEG, D), BF16),
             pltpu.VMEM((SEG, D), BF16), pltpu.VMEM((D, D), BF16),
-            pltpu.SemaphoreType.DMA((5,)),
+            pltpu.SMEM((1, SLIDES), jnp.int32),
+            pltpu.SemaphoreType.DMA((6,)),
             pltpu.VMEM((3, SEG, D), BF16),
             pltpu.SemaphoreType.DMA((3,)),
             heads(NHEAD, BF16), heads(NHEAD, BF16), heads(NHEAD, BF16), heads(NHEAD, BF16),
@@ -654,12 +662,14 @@
     return pl.pallas_call(
         final_kernel,
         out_shape=(out, out, out, jax.ShapeDtypeStruct((z_rows, COLS), F32)),
-        in_specs=[pl.BlockSpec(memory_space=pl.ANY), vmem],
-        out_specs=(pl.BlockSpec(memory_space=pl.ANY),) * 3 + (vmem,),
+        in_specs=[pl.BlockSpec(memory_space=pl.ANY)] * 2,
+        out_specs=(pl.BlockSpec(memory_space=pl.ANY),) * 4,
         scratch_shapes=[
             pltpu.VMEM((3, SEG, D), BF16),
-            pltpu.SemaphoreType.DMA((3,)),
-            pltpu.SemaphoreType.DMA((3,)),
+            pltpu.VMEM((z_pad, 128), F32),
+            pltpu.VMEM((z_rows, COLS), F32),
+            pltpu.SemaphoreType.DMA((4,)),
+            pltpu.SemaphoreType.DMA((4,)),
         ],
         compiler_params=pltpu.CompilerParams(vmem_limit_bytes=VMEM_LIMIT),
     )(grads, partial)

time: 49.9 us -> 47.9 us (0.960)
  Pallas kernels: 48.6 us -> 46.7 us
    pallas_call x1, Pallas kernels: 3.35 us -> 2.07 us  [on_device(): pl.pallas_call(final_kernel, out_shape=(out, out, out, jax.ShapeDtypeStru...]
    pallas_call x1, Pallas kernels: 45.3 us -> 44.6 us  [on_device(): pl.pallas_call(kernel, out_shape=(jax.ShapeDtypeStruct((3, SEG, D), BF16)...]
where the time goes in v5:
time: 47.9 us; the launch traced here: 47.3 us
  Pallas kernels  46.7 us (97%)
  between operations  0.64 us (1%)
    pallas_call x1, Pallas kernels, on_device(): pl.pallas_call(kernel, out_shape=(jax.ShapeDtypeStruct((3, SEG, D), BF16)...  44.6 us
    pallas_call x1, Pallas kernels, on_device(): pl.pallas_call(final_kernel, out_shape=(out, out, out, jax.ShapeDtypeStru...  2.07 us

profile of v5, /device:TPU:1, one launch (start us, length us, event | category | flops | bytes accessed | tf_op | source)
XLA Modules:
  0.0 47.3 jit_solution(11575462544945175475)
XLA Ops:
  0.6 44.6 %shard_map.93 = (bf16[3,256,768]{2,1,0:T(8,128)(2,1)}, f32[16,128]{1,0:T(8,128)}) custom-call(bf16[256,768]{1,0:T(8,128)(2,1)} %q_in.1, bf16[256,768]{1,0:T(8,128)(2,1)} %k_in.1, bf16[256,768]{1,0:T(8,128)(2,1)} %v_in.1, bf16[256,768]{1,0:T(8,128)(2,1)} %g_in.1, bf16[768,768]{1,0:T(8,128)(2,1)} %w_in.1, s32[1,4]{1,0:T(1,128)} %len_in.1), custom_call_target="tpu_custom_call" | custom-call | tf_op jit(solution)/shard_map/pallas_call | solution.py:610
  45.3 2.1 %shard_map.94 = (bf16[256,768]{1,0:T(8,128)(2,1)}, bf16[256,768]{1,0:T(8,128)(2,1)}, bf16[256,768]{1,0:T(8,128)(2,1)}, f32[12,96]{1,0:T(8,128)}) custom-call(bf16[3,256,768]{2,1,0:T(8,128)(2,1)} %get-tuple-element.6.grads_ref, f32[16,128]{1,0:T(8,128)} %get-tuple-element.7.part_ref), custom_call_target="tpu_custom_call" | custom-call | tf_op jit(solution)/shard_map/pallas_call | solution.py:662

commit v6 on v5

--- a/solution.py
+++ b/solution.py
@@ -243,9 +243,11 @@
 
         return start, finish, sent
 
-    def plane_each(do, own=None):
+    def plane_each(do, own=None, first=None):
         for d in (2, 1, 3, 0):
             y = lax.rem(my + d, NY)
+            if first is not None:
+                first(y)
             for b in range(NX):
                 other = 4 * mc + b
                 copy = pltpu.make_async_remote_copy(
@@ -474,33 +476,18 @@
     lse, w_a, w_b = combine(mc, lse_own[...], att)
     combine(1 - mc, lse_x[...], att_x)
 
-    def part(first, count):
-        out = 0.0
-        for rows, cols in (
-            (att, ogt.at[pl.ds(pl.multiple_of(mc * COLH, 128), COLH)]),
-            (att_x, og_x),
-        ):
-            starts = [y * (MAIN + REM) + first for y in range(NY)]
-            x = jnp.concatenate([rows[i : i + count] for i in starts], 0)
-            out = out + mm_nt(cols[...], x)
-        return out
-
     zz = along(NZ, mz, lambda z: (my * NZ + z, me), z_send, z_recv, z_sem)
-    main, rest = part(0, MAIN), part(MAIN, REM)
-    low = iota((COLS // 2, 128), 1) < REM
-    for y in range(NY):
+    def block_of(y):
+        rows = pl.ds(pl.multiple_of(y * (MAIN + REM), REM), MAIN + REM)
+        cols = pl.ds(pl.multiple_of(mc * COLH, 128), COLH)
+        out = mm_nt(ogt[cols], att[rows]) + mm_nt(og_x[...], att_x[rows])
         for b in range(NX):
-            d_send[y * NX + b, :COLS] = main[
-                b * COLS : (b + 1) * COLS, y * MAIN : (y + 1) * MAIN
-            ].astype(BF16)
-            x = rest[b * COLS : (b + 1) * COLS, y // 2 * 128 : y // 2 * 128 + 128]
-            top, bottom = x[: COLS // 2], x[COLS // 2 :]
-            if y % 2:
-                top = pltpu.roll(top, REM, 1)
-            else:
-                bottom = pltpu.roll(bottom, REM, 1)
-            d_send[y * NX + b, COLS:] = jnp.where(low, top, bottom).astype(BF16)
-    plane_each(lambda copy: copy.start(), plane_own)
+            x = out[b * COLS : (b + 1) * COLS]
+            rest = jnp.concatenate([x[: COLS // 2, MAIN:], x[COLS // 2 :, MAIN:]], 1)
+            d_send[y * NX + b, :COLS] = x[:, :MAIN].astype(BF16)
+            d_send[y * NX + b, COLS:] = rest.astype(BF16)
+
+    plane_each(lambda copy: copy.start(), plane_own, block_of)
 
     arrive(4, send4, recv4)
     pairs = []

time: 47.9 us -> 47.7 us (level)
  no operation moved by 1% of the time
where the time goes in v6:
time: 47.7 us; the launch traced here: 47.3 us
  Pallas kernels  46.7 us (98%)
  between operations  0.64 us (1%)
    pallas_call x1, Pallas kernels, on_device(): pl.pallas_call(kernel, out_shape=(jax.ShapeDtypeStruct((3, SEG, D), BF16)...  44.6 us
    pallas_call x1, Pallas kernels, on_device(): pl.pallas_call(final_kernel, out_shape=(out, out, out, jax.ShapeDtypeStru...  2.07 us

profile of v6, /device:TPU:1, one launch (start us, length us, event | category | flops | bytes accessed | tf_op | source)
XLA Modules:
  0.0 47.3 jit_solution(5665813231370035962)
XLA Ops:
  0.6 44.6 %shard_map.93 = (bf16[3,256,768]{2,1,0:T(8,128)(2,1)}, f32[16,128]{1,0:T(8,128)}) custom-call(bf16[256,768]{1,0:T(8,128)(2,1)} %q_in.1, bf16[256,768]{1,0:T(8,128)(2,1)} %k_in.1, bf16[256,768]{1,0:T(8,128)(2,1)} %v_in.1, bf16[256,768]{1,0:T(8,128)(2,1)} %g_in.1, bf16[768,768]{1,0:T(8,128)(2,1)} %w_in.1, s32[1,4]{1,0:T(1,128)} %len_in.1), custom_call_target="tpu_custom_call" | custom-call | tf_op jit(solution)/shard_map/pallas_call | solution.py:597
  45.2 2.1 %shard_map.94 = (bf16[256,768]{1,0:T(8,128)(2,1)}, bf16[256,768]{1,0:T(8,128)(2,1)}, bf16[256,768]{1,0:T(8,128)(2,1)}, f32[12,96]{1,0:T(8,128)}) custom-call(bf16[3,256,768]{2,1,0:T(8,128)(2,1)} %get-tuple-element.6.grads_ref, f32[16,128]{1,0:T(8,128)} %get-tuple-element.7.part_ref), custom_call_target="tpu_custom_call" | custom-call | tf_op jit(solution)/shard_map/pallas_call | solution.py:649
